TPU v7x, 32 devices: a whole 2x2x4 slice. The times are simulated.
32 devices in a mesh: head: 4 (over x, core), blk: 8 (over z, y).
Axes of the slice: x: 2, y: 2, z: 4, core: 2. Of those that a mesh axis runs over, the one named last changes fastest.
Arguments:
- query: bfloat16 [4096, 4096], P(('blk', 'head')), may hold values from -6 to 6
- keys: bfloat16 [4096, 1024], P(('blk', 'head')), may hold values from -6 to 6
- values: bfloat16 [4096, 1024], P(('blk', 'head')), may hold values from -6 to 6
- forward_out: bfloat16 [4096, 4096], P(('blk', 'head')), may hold values from -6 to 6
- out_grad: bfloat16 [4096, 4096], P(('blk', 'head')), may hold values from -6 to 6
- log_norm: float32 [32, 4096], P(None, ('blk', 'head')), may hold values from 3 to 5
- tile_mask: int32 [8, 4, 4, 4], P('blk'), may hold values 0 or 1
Outputs:
- query_grad: bfloat16 [4096, 4096], P(('blk', 'head'))
- keys_grad: bfloat16 [4096, 1024], P(('blk', 'head'))
- values_grad: bfloat16 [4096, 1024], P(('blk', 'head'))
All inputs are finite; a program needn't handle non-finite values. No bound on the sum of `tile_mask` on one device may be relied on, other than what follows from the above.
Results may differ from a plain program's by a relative error of at most 0.005.
Values may be sent and summed in bfloat16 or wider, within the bound.
No kernel may reach another device: no remote copies, remote signals or barrier semaphores. Data moves between devices by JAX's collectives and lax.ppermute only.
A program may use at most 128 MiB of HBM per device.

v0:
```python
import functools

import jax
import jax.numpy as jnp
from jax import lax
from jax.experimental import pallas as pl
from jax.experimental.pallas import tpu as pltpu
from jax.sharding import Mesh
from jax.sharding import PartitionSpec as P

HD = 128
STEPS = 4
SCALE = HD ** (-0.5)
LOG2E = 1.4426950408889634
F32 = jnp.float32
BF16 = jnp.bfloat16
EXTRA = 32
UNROLL = 4
PIPELINED = False
VMEM_LIMIT = 16 * 1024 * 1024
VMEM_ALL = 60 * 1024 * 1024

WHOLE = pl.BlockSpec(memory_space=pltpu.VMEM)
ANYWHERE = pl.BlockSpec(memory_space=pl.ANY)
SCALARS = pl.BlockSpec(memory_space=pltpu.SMEM)


def dot(a, b, dims):
    return lax.dot_general(a, b, (dims, ((), ())), preferred_element_type=F32)


def pack_kv(keys, values, tile_mask, parts):
    tokens = keys.shape[0]
    steps, tiles = tile_mask.shape[1:3]

    def kernel(k_ref, v_ref, m_ref, out_ref, mask):
        mask[...] = jnp.zeros_like(mask)
        for step in range(steps):
            mask[step * tiles : (step + 1) * tiles, :tiles] = m_ref[0, step].astype(F32)
        for g in range(parts):
            out_ref[g, :tokens, :] = k_ref[:, g * HD : (g + 1) * HD]
            out_ref[g, tokens : 2 * tokens, :] = v_ref[:, g * HD : (g + 1) * HD]
            out_ref[g, 2 * tokens :, :] = mask[...].astype(BF16)

    return pl.pallas_call(
        kernel,
        out_shape=jax.ShapeDtypeStruct((parts, 2 * tokens + steps * tiles, HD), keys.dtype),
        in_specs=[WHOLE, WHOLE, WHOLE],
        out_specs=WHOLE,
        scratch_shapes=[pltpu.VMEM((steps * tiles, HD), F32)],
        name="pack_kv",
    )(keys, values, tile_mask)


def split3(x):
    a = x.astype(BF16)
    r = x - a.astype(F32)
    b = r.astype(BF16)
    c = (r - b.astype(F32)).astype(BF16)
    return a, b, c


def pack_queries(me, query, out_grad, forward_out, log_norm, parts):
    tokens = query.shape[0]
    heads = log_norm.shape[0] // parts
    width = heads * HD
    rows = 2 * heads * tokens + EXTRA

    def kernel(me_ref, q_ref, g_ref, f_ref, n_ref, *refs):
        outs = refs[:parts]
        q_buf, g_buf, f_buf, n_buf, sem, n_sem = refs[parts:]
        n_load = pltpu.make_async_copy(n_ref, n_buf, n_sem)
        n_load.start()
        loads = []
        for d in range(parts):
            start = jnp.bitwise_xor(me_ref[0], d) * width
            lanes = pl.ds(pl.multiple_of(start, width), width)
            loads.append(
                [
                    pltpu.make_async_copy(ref.at[:, lanes], buf.at[d], sem.at[i, d])
                    for i, (ref, buf) in enumerate(((g_ref, g_buf), (f_ref, f_buf), (q_ref, q_buf)))
                ]
            )
            for copy in loads[d]:
                copy.start()
        line = lax.broadcasted_iota(jnp.int32, (16, width), 0)
        lane = lax.broadcasted_iota(jnp.int32, (16, width), 1)
        pick = jnp.where(lane // HD == line, 1.0, 0.0).astype(BF16)
        pad = jnp.zeros((EXTRA - 6 * heads, tokens), BF16)
        n_load.wait()
        for d, out in enumerate(outs):
            for copy in loads[d]:
                copy.wait()
            prod = g_buf[d].astype(F32) * f_buf[d].astype(F32)
            high = prod.astype(BF16)
            low = (prod - high.astype(F32)).astype(BF16)
            delta = (dot(pick, high, ((1,), (1,))) + dot(pick, low, ((1,), (1,))))[:heads]
            norm = n_buf[jnp.bitwise_xor(me_ref[0], d)]
            for h in range(heads):
                out[h * tokens : (h + 1) * tokens, :] = q_buf[d, :, h * HD : (h + 1) * HD]
                out[(heads + h) * tokens : (heads + h + 1) * tokens, :] = g_buf[d, :, h * HD : (h + 1) * HD]
            out[2 * heads * tokens :, :] = jnp.concatenate(split3(norm) + split3(delta) + (pad,), axis=0)

    return pl.pallas_call(
        kernel,
        out_shape=[jax.ShapeDtypeStruct((rows, HD), BF16)] * parts,
        in_specs=[SCALARS] + [ANYWHERE] * 4,
        out_specs=[WHOLE] * parts,
        scratch_shapes=[pltpu.VMEM((parts, tokens, width), BF16)] * 3
        + [
            pltpu.VMEM((parts, heads, tokens), F32),
            pltpu.SemaphoreType.DMA((3, parts)),
            pltpu.SemaphoreType.DMA,
        ],
        compiler_params=pltpu.CompilerParams(vmem_limit_bytes=VMEM_ALL),
        name="pack_queries",
    )(me, query, out_grad, forward_out, log_norm.reshape(parts, heads, tokens))


def side_by_side(x):
    return jnp.concatenate([x[h : h + 1] for h in range(x.shape[0])], axis=1)


def terms(where, masks, work, queries, kvs, dq_in, acc_in, dq_done, acc_done, tiles, heads):
    shards_in = [d for d, _ in work]
    names = [n for n in ("own", "one", "two") if any(n in use for _, use in work)]
    tokens = (queries[shards_in[0]].shape[0] - EXTRA) // (2 * heads)
    rows = heads * tokens
    dq_given = [d for d in shards_in if d in dq_in]
    acc_given = [n for n in names if n in acc_in]
    operands = [queries[d] for d in shards_in] + [kvs[n] for n in names]
    operands += [dq_in[d] for d in dq_given] + [acc_in[n] for n in acc_given]
    dq_shapes = [
        jax.ShapeDtypeStruct((rows, HD), BF16) if d in dq_done else jax.ShapeDtypeStruct((HD, rows), F32)
        for d in shards_in
    ]
    sizes = {n: kvs[n].shape[0] for n in names}
    starts = {n: sum(sizes[m] for m in names[:i]) for i, n in enumerate(names)}
    total = sum(sizes.values())
    acc_shapes = [jax.ShapeDtypeStruct((sizes[n], tokens, 2 * HD), BF16 if n in acc_done else F32) for n in names]
    longest = sum(2 * tiles * len(use) + UNROLL for _, use in work) + 4 * UNROLL
    block = UNROLL * tokens
    scratch = [
        pltpu.VMEM((len(work), 2 * rows, HD), BF16),
        pltpu.VMEM((len(work), 2, rows), F32),
        pltpu.VMEM((total, 2 * tokens, HD), BF16),
        pltpu.VMEM((total, tokens, 2 * HD), F32),
        pltpu.VMEM((len(work), HD, rows), F32),
        pltpu.SMEM((longest,), jnp.int32),
        pltpu.SMEM((longest,), F32),
        pltpu.SMEM((longest,), jnp.int32),
    ] + [pltpu.VMEM((block, rows), F32)] * (4 if PIPELINED else 0)

    def kernel(where_ref, mask_ref, *refs):
        refs = list(refs)
        take = lambda keys: {k: refs.pop(0) for k in keys}
        q_refs, kv_refs, dq_old, acc_old = take(shards_in), take(names), take(dq_given), take(acc_given)
        dq_out, acc_out = take(shards_in), take(names)
        q_buf, line_buf, kv_buf, acc, dq_acc, todo, penalty, shard_of = refs[:8]
        pair, head = where_ref[0], where_ref[1]
        for n in names:
            here = pl.ds(starts[n], sizes[n])
            kv_buf[here] = kv_refs[n][:, : 2 * tokens, :]
            acc[here] = acc_old[n][...] if n in acc_old else jnp.zeros((sizes[n], tokens, 2 * HD), F32)

        place = jnp.int32(0)
        for slot, (d, use) in enumerate(work):
            q_ref = q_refs[d]
            q_buf[slot] = q_ref[: 2 * rows, :]
            extra = q_ref[2 * rows :, :].astype(F32)
            piece = lambda k: extra[k * heads : (k + 1) * heads]
            line_buf[slot, 0:1, :] = side_by_side(piece(0) + piece(1) + piece(2)) * LOG2E
            line_buf[slot, 1:2, :] = side_by_side(piece(3) + piece(4) + piece(5))
            dq_acc[slot] = dq_old[d][...] if d in dq_old else jnp.zeros((HD, rows), F32)
            other = jnp.bitwise_xor(pair, d // tiles)
            row = jnp.bitwise_xor(head, d % tiles)

            def seen(step, j):
                return mask_ref[other, step * tiles * tiles + row * tiles + j]

            wanted = []
            if "own" in use:
                wanted += [(starts["own"] + j, seen(other, j)) for j in range(tiles)]
                wanted += [(starts["own"] + tiles + j, seen(0, j) * other) for j in range(tiles)]
            if "one" in use:
                wanted += [(starts["one"] + j, seen(2 + other, j)) for j in range(tiles)]
                wanted += [(starts["one"] + tiles + j, seen(1 + other, j)) for j in range(tiles)]
            if "two" in use:
                wanted += [(starts["two"] + j, seen(3, j) * (1 - other)) for j in range(tiles)]
            begin = place
            for tile, flag in wanted:
                todo[place] = jnp.int32(tile)
                penalty[place] = 0.0
                place = place + flag
            for u in range(UNROLL - 1):
                todo[place + u] = jnp.int32(0)
                penalty[place + u] = 1e30
            place = begin + (place - begin + UNROLL - 1) // UNROLL * UNROLL
            for g in range((len(wanted) + UNROLL - 1) // UNROLL):
                shard_of[begin // UNROLL + g] = jnp.int32(slot)
        groups = place // UNROLL
        for u in range(2 * UNROLL):
            todo[place + u] = jnp.int32(0)
            penalty[place + u] = 1e30
        shard_of[groups] = jnp.int32(0)
        shard_of[groups + 1] = jnp.int32(0)

        def load(g):
            slot = shard_of[g]
            spots = [todo[g * UNROLL + u] for u in range(UNROLL)]
            k = jnp.concatenate([kv_buf[t, :tokens, :] for t in spots], axis=0)
            return slot, spots, k

        def before(g):
            slot, spots, k = load(g)
            v = jnp.concatenate([kv_buf[t, tokens:, :] for t in spots], axis=0)
            return dot(k, q_buf[slot, :rows, :], ((1,), (1,))), dot(v, q_buf[slot, rows:, :], ((1,), (1,)))

        def after(g, score, dprob):
            slot, spots, k = load(g)
            lines = line_buf[slot]
            prob = jnp.concatenate(
                [
                    jnp.exp2(
                        score[u * tokens : (u + 1) * tokens] * (SCALE * LOG2E)
                        - (lines[0:1] + penalty[g * UNROLL + u])
                    )
                    for u in range(UNROLL)
                ],
                axis=0,
            )
            dscore = (prob * (dprob - lines[1:2])).astype(BF16)
            dv = dot(prob.astype(BF16), q_buf[slot, rows:, :], ((1,), (0,)))
            dk = dot(dscore, q_buf[slot, :rows, :], ((1,), (0,)))
            dq_acc[slot] += dot(k, dscore, ((0,), (0,)))
            for u, t in enumerate(spots):
                acc[t, :, :HD] += dk[u * tokens : (u + 1) * tokens]
                acc[t, :, HD:] += dv[u * tokens : (u + 1) * tokens]

        if PIPELINED:
            s0, p0, s1, p1 = refs[8:]
            s0[...], p0[...] = before(0)

            def body(i, carry):
                g = 2 * i
                s1[...], p1[...] = before(g + 1)
                after(g, s0[...], p0[...])
                s0[...], p0[...] = before(g + 2)
                after(g + 1, s1[...], p1[...])
                return carry

            lax.fori_loop(0, (groups + 1) // 2, body, 0)
        else:

            def body(g, carry):
                after(g, *before(g))
                return carry

            lax.fori_loop(0, groups, body, 0)

        for slot, d in enumerate(shards_in):
            if d in dq_done:
                dq_out[d][...] = (dq_acc[slot] * SCALE).T.astype(BF16)
            else:
                dq_out[d][...] = dq_acc[slot]
        for n in names:
            acc_out[n][...] = acc[pl.ds(starts[n], sizes[n])].astype(acc_out[n].dtype)

    outs = pl.pallas_call(
        kernel,
        out_shape=dq_shapes + acc_shapes,
        in_specs=[SCALARS, SCALARS] + [WHOLE] * len(operands),
        out_specs=[WHOLE] * (len(dq_shapes) + len(names)),
        scratch_shapes=scratch,
        compiler_params=pltpu.CompilerParams(vmem_limit_bytes=VMEM_LIMIT),
        cost_estimate=pl.CostEstimate(
            flops=10 * sum(len(use) for _, use in work) * rows * tiles * tokens * HD,
            bytes_accessed=sum(x.size * 2 for x in operands),
            transcendentals=0,
        ),
        name="terms",
    )(where, masks, *operands)
    return dict(zip(shards_in, outs)), dict(zip(names, outs[len(shards_in) :]))


def total_kv(own, one, two, after):
    tiles = two.shape[0]

    def kernel(own_ref, one_ref, two_ref, *refs):
        out_ref = refs[-1]
        for t in range(2 * tiles):
            total = own_ref[t] + one_ref[t].astype(F32)
            if t >= tiles:
                total = total + two_ref[t - tiles].astype(F32)
            out_ref[t, :, :HD] = (total[:, :HD] * SCALE).astype(BF16)
            out_ref[t, :, HD:] = total[:, HD:].astype(BF16)

    return pl.pallas_call(
        kernel,
        out_shape=jax.ShapeDtypeStruct(own.shape, BF16),
        in_specs=[WHOLE] * 3 + [ANYWHERE] * len(after),
        out_specs=WHOLE,
        name="total_kv",
    )(own, one, two, *after)


def unpack_queries(me, grads, tokens):
    parts = len(grads)
    heads = grads[0].shape[0] // tokens
    width = heads * HD

    def kernel(me_ref, *refs):
        out = refs[parts]
        for d in range(parts):
            source = jnp.bitwise_xor(me_ref[0], d)
            for h in range(heads):
                out[:, pl.ds(pl.multiple_of(source * width + h * HD, HD), HD)] = refs[d][h * tokens : (h + 1) * tokens, :]

    return pl.pallas_call(
        kernel,
        out_shape=jax.ShapeDtypeStruct((tokens, parts * width), BF16),
        in_specs=[SCALARS] + [WHOLE] * parts,
        out_specs=WHOLE,
        name="unpack_queries",
    )(me, *grads)


def unpack_kv(grads):
    parts, tokens = grads.shape[:2]

    def kernel(in_ref, k_ref, v_ref):
        for g in range(parts):
            k_ref[:, g * HD : (g + 1) * HD] = in_ref[g, :, :HD]
            v_ref[:, g * HD : (g + 1) * HD] = in_ref[g, :, HD:]

    return pl.pallas_call(
        kernel,
        out_shape=[jax.ShapeDtypeStruct((tokens, parts * HD), BF16)] * 2,
        in_specs=[WHOLE],
        out_specs=[WHOLE] * 2,
        name="unpack_kv",
    )(grads)


def shards(sizes, query, keys, values, forward_out, out_grad, log_norm, tile_mask):
    n_head, n_sup, n_pair = sizes
    parts = n_head * n_pair
    tiles = tile_mask.shape[-1]
    tokens = query.shape[0]
    heads = log_norm.shape[0] // parts
    pair, head = lax.axis_index("pair"), lax.axis_index("head")
    me = (pair * n_head + head).astype(jnp.int32).reshape(1)
    where = jnp.stack([pair, head]).astype(jnp.int32)

    def swap(value, d):
        far, near = d // n_head, d % n_head
        pairs = [
            (h * n_pair + p, (h ^ near) * n_pair + (p ^ far)) for h in range(n_head) for p in range(n_pair)
        ]
        return lax.ppermute(value, ("head", "pair"), pairs)

    def along(value, steps):
        return lax.ppermute(value, "sup", [(i, (i + steps) % n_sup) for i in range(n_sup)])

    def exchange(value):
        return lax.all_to_all(value, ("pair", "head"), split_axis=0, concat_axis=0, tiled=True)

    kv_own = exchange(pack_kv(keys, values, tile_mask, parts))
    packed = pack_queries(me, query, out_grad, forward_out, log_norm, parts)
    first = [0, 1, 2, n_head]
    last = [parts - 2, parts - 1]
    middle = [d for d in range(parts) if d not in first + last]
    queries = {d: swap(packed[d], d) if d else packed[d] for d in first}
    held, kv_own = lax.optimization_barrier(([packed[d] for d in middle], kv_own))
    kvs = {"own": kv_own, "one": along(kv_own, 1), "two": along(kv_own[n_head:], 2)}
    queries.update({d: swap(x, d) for d, x in zip(middle, held)})
    held, arrived = lax.optimization_barrier(([packed[d] for d in last], [queries[d] for d in first[2:]]))
    queries.update(dict(zip(first[2:], arrived)))
    queries.update({d: swap(x, d) for d, x in zip(last, held)})
    masks = kv_own[::n_head, 2 * tokens :, :tiles].astype(jnp.int32).reshape(n_pair, -1)
    args = dict(tiles=tiles, heads=heads)
    call = lambda work, dq, acc, dq_done, acc_done: terms(
        where, masks, work, queries, kvs, dq, acc, dq_done, acc_done, **args
    )
    dq, sums = call([(d, ["own"]) for d in first], {}, {}, [], [])
    some, sums = call([(d, ["one"]) for d in first] + [(d, ["own", "one"]) for d in middle], dq, sums, [], [])
    dq.update(some)
    some, sums = call([(d, ["own", "one"]) for d in last], {}, sums, [], ["one"])
    dq.update(some)
    one = along(sums["one"], -1)
    grads, two = call([(d, ["two"]) for d in range(parts)], dq, {}, list(range(parts)), ["two"])
    two = along(two["two"], -2)
    grads = [swap(grads[d], d) if d else grads[d] for d in range(parts)]
    kv_grad = exchange(total_kv(sums["own"], one, two, grads[1:]))
    query_grad = unpack_queries(me, grads, tokens)
    keys_grad, values_grad = unpack_kv(kv_grad)
    return query_grad, keys_grad, values_grad


def solution(mesh):
    sizes = dict(mesh.shape)
    n_head, n_blk = sizes["head"], sizes["blk"]
    n_pair = 2
    devices = mesh.devices
    if tuple(mesh.axis_names) != ("head", "blk"):
        raise ValueError("mesh axes")
    n_sup = n_blk // n_pair
    finer = Mesh(devices.reshape(n_head, n_sup, n_pair), ("head", "sup", "pair"))
    tokens = P(("sup", "pair", "head"), None)
    in_specs = (tokens,) * 5 + (P(None, ("sup", "pair", "head")), P(("sup", "pair"), None, None, None))
    return jax.shard_map(
        functools.partial(shards, (n_head, n_sup, n_pair)),
        mesh=finer,
        in_specs=in_specs,
        out_specs=(tokens,) * 3,
        check_vma=False,
    )
```

profile of v0, /device:TPU:0, one launch (start us, length us, event | category | flops | bytes accessed | tf_op | source)
XLA Modules:
  0.0 102.2 jit_solution(13930804546233332085)
XLA Ops:
  0.6 1.9 %pack_kv.1 = bf16[8,272,128]{2,1,0:T(8,128)(2,1)} custom-call(bf16[128,1024]{1,0:T(8,128)(2,1)} %k_ref.1, bf16[128,1024]{1,0:T(8,128)(2,1)} %v_ref.1, s32[1,4,4,4]{3,2,1,0:T(4,128)} %m_ref.1), custom_call_target="tpu_custom_call" | custom-call | tf_op jit(solution)/shard_map/pack_kv/pallas_call | solution.py:45
  2.6 5.2 %all-to-all-start = ((bf16[8,272,128]{2,1,0:T(8,128)(2,1)}), bf16[8,272,128]{2,1,0:T(8,128)(2,1)S(1)}, u32[]{:S(2)}, u32[]{:S(2)}) async-start(bf16[8,272,128]{2,1,0:T(8,128)(2,1)} %pack_kv.1), calls=%async_computation | async-start | bytes 1114112 | tf_op jit(solution)/shard_map/all_to_all | solution.py:366
  7.7 5.5 %pack_queries.1 = (bf16[1056,128]{1,0:T(8,128)(2,1)}, bf16[1056,128]{1,0:T(8,128)(2,1)}, bf16[1056,128]{1,0:T(8,128)(2,1)}, bf16[1056,128]{1,0:T(8,128)(2,1)}, b...) custom-call(s32[1]{0:T(128)} %bitcast.me_ref, ...), custom_call_target="tpu_custom_call" | custom-call | tf_op jit(solution)/shard_map/pack_queries/pallas_call | solution.py:104
  13.3 2.1 %collective-permute-start.1 = (bf16[1056,128]{1,0:T(8,128)(2,1)}, bf16[1056,128]{1,0:T(8,128)(2,1)S(1)}, u32[]{:S(2)}, u32[]{:S(2)}) collective-permute-start(bf16[1056,128]{1,0:T(8,128)(2,1)} %get-tuple-element.53), channel_id=1, source_target_pairs={{0,16},{1,17},{8,24},{9,25},{16,0},{17,1},{24,8},{25,9},{2,18},{3,... | collective-permute-start | bytes 811016 | tf_op jit(solution)/shard_map/ppermute | solution.py:360
  15.4 1.5 %collective-permute-start.2 = (bf16[1056,128]{1,0:T(8,128)(2,1)}, bf16[1056,128]{1,0:T(8,128)(2,1)S(1)}, u32[]{:S(2)}, u32[]{:S(2)}) collective-permute-start(bf16[1056,128]{1,0:T(8,128)(2,1)} %get-tuple-element.54), channel_id=1, source_target_pairs={{0,1},{1,0},{8,9},{9,8},{16,17},{17,16},{24,25},{25,24},{2,3},{3,2... | collective-permute-start | bytes 811016 | tf_op jit(solution)/shard_map/ppermute | solution.py:360
  16.8 1.0 all-to-all-done.refs_4_.refs_6_.refs_2_
  17.8 1.6 %collective-permute-start.8 = (bf16[8,272,128]{2,1,0:T(8,128)(2,1)S(1)}, bf16[8,272,128]{2,1,0:T(8,128)(2,1)S(1)}, u32[]{:S(2)}, u32[]{:S(2)}) collective-permute-start(bf16[8,272,128]{2,1,0:T(8,128)(2,1)S(1)} %all-to-all-done.refs_4_.refs_6_.refs_2_), channel_id=1, source_target_pairs={{0,2},{2,4},{4,6},{6,0},{1,3},{3,5},{5,7},{7,1},{8,10},{10,12},{12... | collective-permute-start | bytes 1671176 | tf_op jit(solution)/shard_map/ppermute | solution.py:363
  19.5 3.2 %collective-permute-done.1.refs_2_ = bf16[1056,128]{1,0:T(8,128)(2,1)S(1)} collective-permute-done((bf16[1056,128]{1,0:T(8,128)(2,1)}, bf16[1056,128]{1,0:T(8,128)(2,1)S(1)}, u32[]{:S(2)}, u32[]{:S(2)}) %collective-permute-start.1) | collective-permute-done | bytes 270368 | tf_op jit(solution)/shard_map/ppermute | solution.py:360
  22.7 1.1 %collective-permute-done.2.refs_3_.refs_4_ = bf16[1056,128]{1,0:T(8,128)(2,1)S(1)} collective-permute-done((bf16[1056,128]{1,0:T(8,128)(2,1)}, bf16[1056,128]{1,0:T(8,128)(2,1)S(1)}, u32[]{:S(2)}, u32[]{:S(2)}) %collective-permute-start.2) | collective-permute-done | bytes 270368 | tf_op jit(solution)/shard_map/ppermute | solution.py:360
  23.8 1.5 %collective-permute-start.5 = (bf16[1056,128]{1,0:T(8,128)(2,1)}, bf16[1056,128]{1,0:T(8,128)(2,1)S(1)}, u32[]{:S(2)}, u32[]{:S(2)}) collective-permute-start(bf16[1056,128]{1,0:T(8,128)(2,1)} %get-tuple-element.59), channel_id=1, source_target_pairs={{0,17},{1,16},{8,25},{9,24},{16,1},{17,0},{24,9},{25,8},{2,19},{3,... | collective-permute-start | bytes 811016 | tf_op jit(solution)/shard_map/ppermute | solution.py:360
  25.3 1.7 %collective-permute-start.4 = (bf16[1056,128]{1,0:T(8,128)(2,1)}, bf16[1056,128]{1,0:T(8,128)(2,1)S(1)}, u32[]{:S(2)}, u32[]{:S(2)}) collective-permute-start(bf16[1056,128]{1,0:T(8,128)(2,1)} %get-tuple-element.58), channel_id=1, source_target_pairs={{0,9},{1,8},{8,1},{9,0},{16,25},{17,24},{24,17},{25,16},{2,11},{3,... | collective-permute-start | bytes 811016 | tf_op jit(solution)/shard_map/ppermute | solution.py:360
  27.2 1.0 collective-permute-start.6
  29.1 5.0 %terms.4 = (f32[128,512]{1,0:T(8,128)S(1)}, f32[128,512]{1,0:T(8,128)S(1)}, f32[128,512]{1,0:T(8,128)S(1)}, f32[128,512]{1,0:T(8,128)S(1)}, f32[8,128,256]{2,1,0:T(8,128)S(1)}) custom-call(s32[2]{0:T(128)S(1)} %pad_add_fusion.where_ref, s32[2,64]{1,0:T(2,128)S(1)} %reshape.22.mask_ref, bf16[1056,128]{1,0:T(8,128)(2,1)S(1)} %copy-done.2, ...), custom_call_target="tpu_custom_call" | custom-call | flops 1342177280 | bytes 1638400 | tf_op jit(solution)/shard_map/terms/pallas_call | solution.py:269
  34.1 4.3 %collective-permute-done.3.refs_4_.refs_3_ = bf16[1056,128]{1,0:T(8,128)(2,1)S(1)} collective-permute-done((bf16[1056,128]{1,0:T(8,128)(2,1)}, bf16[1056,128]{1,0:T(8,128)(2,1)S(1)}, u32[]{:S(2)}, u32[]{:S(2)}) %collective-permute-start.3) | collective-permute-done | bytes 270368 | tf_op jit(solution)/shard_map/ppermute | solution.py:360
  38.4 2.6 %collective-permute-start.7 = (bf16[4,272,128]{2,1,0:T(8,128)(2,1)S(1)}, bf16[4,272,128]{2,1,0:T(8,128)(2,1)S(1)}, u32[]{:S(2)}, u32[]{:S(2)}) collective-permute-start(bf16[4,272,128]{2,1,0:T(8,128)(2,1)S(1)} %slice.7), channel_id=1, source_target_pairs={{0,4},{2,6},{4,0},{6,2},{1,5},{3,7},{5,1},{7,3},{8,12},{10,14},{12... | collective-permute-start | bytes 835592 | tf_op jit(solution)/shard_map/ppermute | solution.py:363
  41.0 8.7 %terms.5 = (f32[128,512]{1,0:T(8,128)S(1)}, f32[128,512]{1,0:T(8,128)S(1)}, f32[128,512]{1,0:T(8,128)S(1)}, f32[128,512]{1,0:T(8,128)S(1)}, f32[128,512]{1,0:T(8...) custom-call(s32[2]{0:T(128)S(1)} %pad_add_fusion.where_ref, ...), custom_call_target="tpu_custom_call" | custom-call | flops 2684354560 | bytes 3784704 | tf_op jit(solution)/shard_map/terms/pallas_call | solution.py:269
  49.7 3.4 %terms.6 = (f32[128,512]{1,0:T(8,128)S(1)}, f32[128,512]{1,0:T(8,128)S(1)}, f32[8,128,256]{2,1,0:T(8,128)S(1)}, bf16[8,128,256]{2,1,0:T(8,128)(2,1)S(1)}) custom-call(s32[2]{0:T(128)S(1)} %pad_add_fusion.where_ref, s32[2,64]{1,0:T(2,128)S(1)} %reshape.22.mask_ref, bf16[1056,128]{1,0:T(8,128)(2,1)S(1)} %collective-permute-done.5.refs_0_.refs_6_, ...), custom_call_target="tpu_custom_call" | custom-call | flops 1342177280 | bytes 2703360 | tf_op jit(solution)/shard_map/terms/pallas_call | solution.py:269
  53.1 1.0 copy-done
  54.1 5.8 %collective-permute-start.16 = (bf16[8,128,256]{2,1,0:T(8,128)(2,1)S(1)}, bf16[8,128,256]{2,1,0:T(8,128)(2,1)S(1)}, u32[]{:S(2)}, u32[]{:S(2)}) collective-permute-start(bf16[8,128,256]{2,1,0:T(8,128)(2,1)S(1)} %get-tuple-element.85), channel_id=1, source_target_pairs={{0,6},{2,0},{4,2},{6,4},{1,7},{3,1},{5,3},{7,5},{8,14},{10,8},{12,... | collective-permute-start | bytes 1572872 | tf_op jit(solution)/shard_map/ppermute | solution.py:363
  59.9 4.5 %terms.7 = (bf16[512,128]{1,0:T(8,128)(2,1)S(1)}, bf16[512,128]{1,0:T(8,128)(2,1)S(1)}, bf16[512,128]{1,0:T(8,128)(2,1)S(1)}, bf16[512,128]{1,0:T(8,128)(2,1)S(1...) custom-call(s32[2]{0:T(128)S(1)} %pad_add_fusion.where_ref, ...), custom_call_target="tpu_custom_call" | custom-call | flops 2684354560 | bytes 3489792 | tf_op jit(solution)/shard_map/terms/pallas_call | solution.py:269
  65.1 1.2 %collective-permute-start.10 = (bf16[512,128]{1,0:T(8,128)(2,1)S(1)}, bf16[512,128]{1,0:T(8,128)(2,1)S(1)}, u32[]{:S(2)}, u32[]{:S(2)}) collective-permute-start(bf16[512,128]{1,0:T(8,128)(2,1)S(1)} %get-tuple-element.78), channel_id=1, source_target_pairs={{0,16},{1,17},{8,24},{9,25},{16,0},{17,1},{24,8},{25,9},{2,18},{3,... | collective-permute-start | bytes 393224 | tf_op jit(solution)/shard_map/ppermute | solution.py:360
  66.4 2.2 %collective-permute-start.13 = (bf16[512,128]{1,0:T(8,128)(2,1)S(1)}, bf16[512,128]{1,0:T(8,128)(2,1)S(1)}, u32[]{:S(2)}, u32[]{:S(2)}) collective-permute-start(bf16[512,128]{1,0:T(8,128)(2,1)S(1)} %get-tuple-element.81), channel_id=1, source_target_pairs={{0,9},{1,8},{8,1},{9,0},{16,25},{17,24},{24,17},{25,16},{2,11},{3,... | collective-permute-start | bytes 393224 | tf_op jit(solution)/shard_map/ppermute | solution.py:360
  68.6 2.3 %collective-permute-done.10.refs_2_.refs_1_ = bf16[512,128]{1,0:T(8,128)(2,1)S(1)} collective-permute-done((bf16[512,128]{1,0:T(8,128)(2,1)S(1)}, bf16[512,128]{1,0:T(8,128)(2,1)S(1)}, u32[]{:S(2)}, u32[]{:S(2)}) %collective-permute-start.10) | collective-permute-done | bytes 131104 | tf_op jit(solution)/shard_map/ppermute | solution.py:360
  70.9 1.2 %collective-permute-done.11.refs_3_.refs_2_ = bf16[512,128]{1,0:T(8,128)(2,1)S(1)} collective-permute-done((bf16[512,128]{1,0:T(8,128)(2,1)S(1)}, bf16[512,128]{1,0:T(8,128)(2,1)S(1)}, u32[]{:S(2)}, u32[]{:S(2)}) %collective-permute-start.11) | collective-permute-done | bytes 131104 | tf_op jit(solution)/shard_map/ppermute | solution.py:360
  72.7 2.5 %collective-permute-start.15 = (bf16[512,128]{1,0:T(8,128)(2,1)S(1)}, bf16[512,128]{1,0:T(8,128)(2,1)S(1)}, u32[]{:S(2)}, u32[]{:S(2)}) collective-permute-start(bf16[512,128]{1,0:T(8,128)(2,1)S(1)} %get-tuple-element.83), channel_id=1, source_target_pairs={{0,25},{1,24},{8,17},{9,16},{16,9},{17,8},{24,1},{25,0},{2,27},{3,... | collective-permute-start | bytes 393224 | tf_op jit(solution)/shard_map/ppermute | solution.py:360
  75.5 3.9 %collective-permute-done.14.refs_6_.refs_5_ = bf16[512,128]{1,0:T(8,128)(2,1)S(1)} collective-permute-done((bf16[512,128]{1,0:T(8,128)(2,1)S(1)}, bf16[512,128]{1,0:T(8,128)(2,1)S(1)}, u32[]{:S(2)}, u32[]{:S(2)}) %collective-permute-start.14) | collective-permute-done | bytes 131104 | tf_op jit(solution)/shard_map/ppermute | solution.py:360
  79.3 2.7 %collective-permute-done.15.refs_7_.refs_6_ = bf16[512,128]{1,0:T(8,128)(2,1)S(1)} collective-permute-done((bf16[512,128]{1,0:T(8,128)(2,1)S(1)}, bf16[512,128]{1,0:T(8,128)(2,1)S(1)}, u32[]{:S(2)}, u32[]{:S(2)}) %collective-permute-start.15) | collective-permute-done | bytes 131104 | tf_op jit(solution)/shard_map/ppermute | solution.py:360
  83.9 2.4 %total_kv.1 = bf16[8,128,256]{2,1,0:T(8,128)(2,1)} custom-call(f32[8,128,256]{2,1,0:T(8,128)} %copy-done, bf16[8,128,256]{2,1,0:T(8,128)(2,1)} %copy-done.5, bf16[4,128,256]{2,1,0:T(8,128)(2,1)} %copy-done.13, bf16[512,128]{1,0:T(8,128)(2,1)} %copy-done.12, bf16[512,128]{1,0:T(8,128)(2,1)} %copy-done.6, bf16[512,128]{1,0:T(8,128)(2,1)} %copy-done.7, ...), custom_call_target="tpu_custom_call" | custom-call | tf_op jit(solution)/shard_map/total_kv/pallas_call | solution.py:298
  86.3 3.5 %all-to-all-start.1 = ((bf16[8,128,256]{2,1,0:T(8,128)(2,1)}), bf16[8,128,256]{2,1,0:T(8,128)(2,1)S(1)}, u32[]{:S(2)}, u32[]{:S(2)}) async-start(bf16[8,128,256]{2,1,0:T(8,128)(2,1)} %total_kv.1), calls=%async_computation.1 | async-start | bytes 1048576 | tf_op jit(solution)/shard_map/all_to_all | solution.py:366
  89.8 2.5 %unpack_queries.1 = bf16[128,4096]{1,0:T(8,128)(2,1)} custom-call(s32[1]{0:T(128)} %bitcast.me_ref, bf16[512,128]{1,0:T(8,128)(2,1)} %copy-done.1, bf16[512,128]{1,0:T(8,128)(2,1)} %copy-done.12, bf16[512,128]{1,0:T(8,128)(2,1)} %copy-done.6, bf16[512,128]{1,0:T(8,128)(2,1)} %copy-done.7, bf16[512,128]{1,0:T(8,128)(2,1)} %copy-done.8, ...), custom_call_target="tpu_custom_call" | custom-call | tf_op jit(solution)/shard_map/unpack_queries/pallas_call | solution.py:319
  92.3 7.1 %all-to-all-done.1.in_ref = bf16[8,128,256]{2,1,0:T(8,128)(2,1)S(1)} async-done(((bf16[8,128,256]{2,1,0:T(8,128)(2,1)}), bf16[8,128,256]{2,1,0:T(8,128)(2,1)S(1)}, u32[]{:S(2)}, u32[]{:S(2)}) %all-to-all-start.1) | async-done | bytes 524320 | tf_op jit(solution)/shard_map/all_to_all | solution.py:366
  100.2 2.0 %unpack_kv.1 = (bf16[128,1024]{1,0:T(8,128)(2,1)}, bf16[128,1024]{1,0:T(8,128)(2,1)}) custom-call(bf16[8,128,256]{2,1,0:T(8,128)(2,1)} %copy-done.4), custom_call_target="tpu_custom_call" | custom-call | tf_op jit(solution)/shard_map/unpack_kv/pallas_call | solution.py:336
  (49 shorter events, 5.3 us)
Async XLA Ops:
  2.6 15.3 %all-to-all-start = ((bf16[8,272,128]{2,1,0:T(8,128)(2,1)}), bf16[8,272,128]{2,1,0:T(8,128)(2,1)S(1)}, u32[]{:S(2)}, u32[]{:S(2)}) async-start(bf16[8,272,128]{2,1,0:T(8,128)(2,1)} %pack_kv.1), calls=%async_computation | async-start | bytes 1114112 | tf_op jit(solution)/shard_map/all_to_all | solution.py:366
  13.3 9.4 %collective-permute-start.1 = (bf16[1056,128]{1,0:T(8,128)(2,1)}, bf16[1056,128]{1,0:T(8,128)(2,1)S(1)}, u32[]{:S(2)}, u32[]{:S(2)}) collective-permute-start(bf16[1056,128]{1,0:T(8,128)(2,1)} %get-tuple-element.53), channel_id=1, source_target_pairs={{0,16},{1,17},{8,24},{9,25},{16,0},{17,1},{24,8},{25,9},{2,18},{3,... | collective-permute-start | bytes 811016 | tf_op jit(solution)/shard_map/ppermute | solution.py:360
  15.4 8.5 %collective-permute-start.2 = (bf16[1056,128]{1,0:T(8,128)(2,1)}, bf16[1056,128]{1,0:T(8,128)(2,1)S(1)}, u32[]{:S(2)}, u32[]{:S(2)}) collective-permute-start(bf16[1056,128]{1,0:T(8,128)(2,1)} %get-tuple-element.54), channel_id=1, source_target_pairs={{0,1},{1,0},{8,9},{9,8},{16,17},{17,16},{24,25},{25,24},{2,3},{3,2... | collective-permute-start | bytes 811016 | tf_op jit(solution)/shard_map/ppermute | solution.py:360
  17.8 23.1 %collective-permute-start.8 = (bf16[8,272,128]{2,1,0:T(8,128)(2,1)S(1)}, bf16[8,272,128]{2,1,0:T(8,128)(2,1)S(1)}, u32[]{:S(2)}, u32[]{:S(2)}) collective-permute-start(bf16[8,272,128]{2,1,0:T(8,128)(2,1)S(1)} %all-to-all-done.refs_4_.refs_6_.refs_2_), channel_id=1, source_target_pairs={{0,2},{2,4},{4,6},{6,0},{1,3},{3,5},{5,7},{7,1},{8,10},{10,12},{12... | collective-permute-start | bytes 1671176 | tf_op jit(solution)/shard_map/ppermute | solution.py:363
  19.4 7.7 %collective-permute-start = (bf16[1056,128]{1,0:T(8,128)(2,1)}, bf16[1056,128]{1,0:T(8,128)(2,1)S(1)}, u32[]{:S(2)}, u32[]{:S(2)}) collective-permute-start(bf16[1056,128]{1,0:T(8,128)(2,1)} %get-tuple-element.50), channel_id=1, source_target_pairs={{0,8},{1,9},{8,0},{9,1},{16,24},{17,25},{24,16},{25,17},{2,10},{3,... | collective-permute-start | bytes 811016 | tf_op jit(solution)/shard_map/ppermute | solution.py:360
  23.8 25.8 %collective-permute-start.5 = (bf16[1056,128]{1,0:T(8,128)(2,1)}, bf16[1056,128]{1,0:T(8,128)(2,1)S(1)}, u32[]{:S(2)}, u32[]{:S(2)}) collective-permute-start(bf16[1056,128]{1,0:T(8,128)(2,1)} %get-tuple-element.59), channel_id=1, source_target_pairs={{0,17},{1,16},{8,25},{9,24},{16,1},{17,0},{24,9},{25,8},{2,19},{3,... | collective-permute-start | bytes 811016 | tf_op jit(solution)/shard_map/ppermute | solution.py:360
  25.3 13.1 %collective-permute-start.3 = (bf16[1056,128]{1,0:T(8,128)(2,1)}, bf16[1056,128]{1,0:T(8,128)(2,1)S(1)}, u32[]{:S(2)}, u32[]{:S(2)}) collective-permute-start(bf16[1056,128]{1,0:T(8,128)(2,1)} %get-tuple-element.56), channel_id=1, source_target_pairs={{0,24},{1,25},{8,16},{9,17},{16,8},{17,9},{24,0},{25,1},{2,26},{3,... | collective-permute-start | bytes 811016 | tf_op jit(solution)/shard_map/ppermute | solution.py:360
  25.3 15.7 %collective-permute-start.4 = (bf16[1056,128]{1,0:T(8,128)(2,1)}, bf16[1056,128]{1,0:T(8,128)(2,1)S(1)}, u32[]{:S(2)}, u32[]{:S(2)}) collective-permute-start(bf16[1056,128]{1,0:T(8,128)(2,1)} %get-tuple-element.58), channel_id=1, source_target_pairs={{0,9},{1,8},{8,1},{9,0},{16,25},{17,24},{24,17},{25,16},{2,11},{3,... | collective-permute-start | bytes 811016 | tf_op jit(solution)/shard_map/ppermute | solution.py:360
  27.2 22.5 %collective-permute-start.6 = (bf16[1056,128]{1,0:T(8,128)(2,1)}, bf16[1056,128]{1,0:T(8,128)(2,1)S(1)}, u32[]{:S(2)}, u32[]{:S(2)}) collective-permute-start(bf16[1056,128]{1,0:T(8,128)(2,1)} %get-tuple-element.60), channel_id=1, source_target_pairs={{0,25},{1,24},{8,17},{9,16},{16,9},{17,8},{24,1},{25,0},{2,27},{3,... | collective-permute-start | bytes 811016 | tf_op jit(solution)/shard_map/ppermute | solution.py:360
  28.1 1.0 copy-start.2
  38.4 21.5 %collective-permute-start.7 = (bf16[4,272,128]{2,1,0:T(8,128)(2,1)S(1)}, bf16[4,272,128]{2,1,0:T(8,128)(2,1)S(1)}, u32[]{:S(2)}, u32[]{:S(2)}) collective-permute-start(bf16[4,272,128]{2,1,0:T(8,128)(2,1)S(1)} %slice.7), channel_id=1, source_target_pairs={{0,4},{2,6},{4,0},{6,2},{1,5},{3,7},{5,1},{7,3},{8,12},{10,14},{12... | collective-permute-start | bytes 835592 | tf_op jit(solution)/shard_map/ppermute | solution.py:363
  49.7 10.2 %copy-start.3 = (bf16[1056,128]{1,0:T(8,128)(2,1)S(1)}, bf16[1056,128]{1,0:T(8,128)(2,1)}, u32[]{:S(2)}) copy-start(bf16[1056,128]{1,0:T(8,128)(2,1)} %get-tuple-element.49.refs_0_) | copy-start | bytes 811012
  53.1 1.0 copy-start
  54.1 28.9 %collective-permute-start.16 = (bf16[8,128,256]{2,1,0:T(8,128)(2,1)S(1)}, bf16[8,128,256]{2,1,0:T(8,128)(2,1)S(1)}, u32[]{:S(2)}, u32[]{:S(2)}) collective-permute-start(bf16[8,128,256]{2,1,0:T(8,128)(2,1)S(1)} %get-tuple-element.85), channel_id=1, source_target_pairs={{0,6},{2,0},{4,2},{6,4},{1,7},{3,1},{5,3},{7,5},{8,14},{10,8},{12,... | collective-permute-start | bytes 1572872 | tf_op jit(solution)/shard_map/ppermute | solution.py:363
  65.1 5.8 %collective-permute-start.10 = (bf16[512,128]{1,0:T(8,128)(2,1)S(1)}, bf16[512,128]{1,0:T(8,128)(2,1)S(1)}, u32[]{:S(2)}, u32[]{:S(2)}) collective-permute-start(bf16[512,128]{1,0:T(8,128)(2,1)S(1)} %get-tuple-element.78), channel_id=1, source_target_pairs={{0,16},{1,17},{8,24},{9,25},{16,0},{17,1},{24,8},{25,9},{2,18},{3,... | collective-permute-start | bytes 393224 | tf_op jit(solution)/shard_map/ppermute | solution.py:360
  66.3 5.7 %collective-permute-start.11 = (bf16[512,128]{1,0:T(8,128)(2,1)S(1)}, bf16[512,128]{1,0:T(8,128)(2,1)S(1)}, u32[]{:S(2)}, u32[]{:S(2)}) collective-permute-start(bf16[512,128]{1,0:T(8,128)(2,1)S(1)} %get-tuple-element.79), channel_id=1, source_target_pairs={{0,24},{1,25},{8,16},{9,17},{16,8},{17,9},{24,0},{25,1},{2,26},{3,... | collective-permute-start | bytes 393224 | tf_op jit(solution)/shard_map/ppermute | solution.py:360
  66.3 6.4 %collective-permute-start.12 = (bf16[512,128]{1,0:T(8,128)(2,1)S(1)}, bf16[512,128]{1,0:T(8,128)(2,1)S(1)}, u32[]{:S(2)}, u32[]{:S(2)}) collective-permute-start(bf16[512,128]{1,0:T(8,128)(2,1)S(1)} %get-tuple-element.80), channel_id=1, source_target_pairs={{0,1},{1,0},{8,9},{9,8},{16,17},{17,16},{24,25},{25,24},{2,3},{3,2... | collective-permute-start | bytes 393224 | tf_op jit(solution)/shard_map/ppermute | solution.py:360
  66.4 9.0 %collective-permute-start.13 = (bf16[512,128]{1,0:T(8,128)(2,1)S(1)}, bf16[512,128]{1,0:T(8,128)(2,1)S(1)}, u32[]{:S(2)}, u32[]{:S(2)}) collective-permute-start(bf16[512,128]{1,0:T(8,128)(2,1)S(1)} %get-tuple-element.81), channel_id=1, source_target_pairs={{0,9},{1,8},{8,1},{9,0},{16,25},{17,24},{24,17},{25,16},{2,11},{3,... | collective-permute-start | bytes 393224 | tf_op jit(solution)/shard_map/ppermute | solution.py:360
  70.9 12.2 %copy-start.6 = (bf16[512,128]{1,0:T(8,128)(2,1)}, bf16[512,128]{1,0:T(8,128)(2,1)S(1)}, u32[]{:S(2)}) copy-start(bf16[512,128]{1,0:T(8,128)(2,1)S(1)} %collective-permute-done.10.refs_2_.refs_1_) | copy-start | bytes 393220
  70.9 12.1 %collective-permute-start.17 = (bf16[4,128,256]{2,1,0:T(8,128)(2,1)S(1)}, bf16[4,128,256]{2,1,0:T(8,128)(2,1)S(1)}, u32[]{:S(2)}, u32[]{:S(2)}) collective-permute-start(bf16[4,128,256]{2,1,0:T(8,128)(2,1)S(1)} %get-tuple-element.86), channel_id=1, source_target_pairs={{0,4},{2,6},{4,0},{6,2},{1,5},{3,7},{5,1},{7,3},{8,12},{10,14},{12... | collective-permute-start | bytes 786440 | tf_op jit(solution)/shard_map/ppermute | solution.py:363
  72.1 10.9 %copy-start.7 = (bf16[512,128]{1,0:T(8,128)(2,1)}, bf16[512,128]{1,0:T(8,128)(2,1)S(1)}, u32[]{:S(2)}) copy-start(bf16[512,128]{1,0:T(8,128)(2,1)S(1)} %collective-permute-done.11.refs_3_.refs_2_) | copy-start | bytes 393220
  72.1 7.3 %collective-permute-start.14 = (bf16[512,128]{1,0:T(8,128)(2,1)S(1)}, bf16[512,128]{1,0:T(8,128)(2,1)S(1)}, u32[]{:S(2)}, u32[]{:S(2)}) collective-permute-start(bf16[512,128]{1,0:T(8,128)(2,1)S(1)} %get-tuple-element.82), channel_id=1, source_target_pairs={{0,17},{1,16},{8,25},{9,24},{16,1},{17,0},{24,9},{25,8},{2,19},{3,... | collective-permute-start | bytes 393224 | tf_op jit(solution)/shard_map/ppermute | solution.py:360
  72.7 10.3 %copy-start.8 = (bf16[512,128]{1,0:T(8,128)(2,1)}, bf16[512,128]{1,0:T(8,128)(2,1)S(1)}, u32[]{:S(2)}) copy-start(bf16[512,128]{1,0:T(8,128)(2,1)S(1)} %collective-permute-done.12.refs_4_.refs_3_) | copy-start | bytes 393220
  72.7 9.3 %collective-permute-start.15 = (bf16[512,128]{1,0:T(8,128)(2,1)S(1)}, bf16[512,128]{1,0:T(8,128)(2,1)S(1)}, u32[]{:S(2)}, u32[]{:S(2)}) collective-permute-start(bf16[512,128]{1,0:T(8,128)(2,1)S(1)} %get-tuple-element.83), channel_id=1, source_target_pairs={{0,25},{1,24},{8,17},{9,16},{16,9},{17,8},{24,1},{25,0},{2,27},{3,... | collective-permute-start | bytes 393224 | tf_op jit(solution)/shard_map/ppermute | solution.py:360
  75.4 7.7 %copy-start.9 = (bf16[512,128]{1,0:T(8,128)(2,1)}, bf16[512,128]{1,0:T(8,128)(2,1)S(1)}, u32[]{:S(2)}) copy-start(bf16[512,128]{1,0:T(8,128)(2,1)S(1)} %collective-permute-done.13.refs_5_.refs_4_) | copy-start | bytes 393220
  75.4 6.7 %collective-permute-start.9 = (bf16[512,128]{1,0:T(8,128)(2,1)S(1)}, bf16[512,128]{1,0:T(8,128)(2,1)S(1)}, u32[]{:S(2)}, u32[]{:S(2)}) collective-permute-start(bf16[512,128]{1,0:T(8,128)(2,1)S(1)} %get-tuple-element.77), channel_id=1, source_target_pairs={{0,8},{1,9},{8,0},{9,1},{16,24},{17,25},{24,16},{25,17},{2,10},{3,... | collective-permute-start | bytes 393224 | tf_op jit(solution)/shard_map/ppermute | solution.py:360
  79.3 3.7 %copy-start.10 = (bf16[512,128]{1,0:T(8,128)(2,1)}, bf16[512,128]{1,0:T(8,128)(2,1)S(1)}, u32[]{:S(2)}) copy-start(bf16[512,128]{1,0:T(8,128)(2,1)S(1)} %collective-permute-done.14.refs_6_.refs_5_) | copy-start | bytes 393220
  82.0 1.0 copy-start.11
  82.0 1.0 %copy-start.12 = (bf16[512,128]{1,0:T(8,128)(2,1)}, bf16[512,128]{1,0:T(8,128)(2,1)S(1)}, u32[]{:S(2)}) copy-start(bf16[512,128]{1,0:T(8,128)(2,1)S(1)} %collective-permute-done.9.refs_1_.refs_0_) | copy-start | bytes 393220
  83.0 0.9 copy-start.5
  86.3 13.2 %all-to-all-start.1 = ((bf16[8,128,256]{2,1,0:T(8,128)(2,1)}), bf16[8,128,256]{2,1,0:T(8,128)(2,1)S(1)}, u32[]{:S(2)}, u32[]{:S(2)}) async-start(bf16[8,128,256]{2,1,0:T(8,128)(2,1)} %total_kv.1), calls=%async_computation.1 | async-start | bytes 1048576 | tf_op jit(solution)/shard_map/all_to_all | solution.py:366
  99.4 0.8 copy-start.4
  (2 other events, 1.4 us)
where the time goes:
time: 104 us; the launch traced here: 102 us
  Pallas kernels  36 us (35%)
  starting transfers between devices  32.7 us (31%)
  waiting for transfers between devices  28.4 us (27%)
  local copies, waits for them, and re-layouts  4.32 us (4%)
    pallas_call x4, Pallas kernels, terms(): pl.pallas_call(kernel, out_shape=dq_shapes + acc_shapes, in_specs=[SCALAR...  21.6 us
    ppermute x14, waiting for transfers between devices, swap(): return lax.ppermute(value, ('head', 'pair'), pairs)  19.3 us
    ppermute x14, starting transfers between devices, swap(): return lax.ppermute(value, ('head', 'pair'), pairs)  14 us
    ppermute x4, starting transfers between devices, along(): lax.ppermute(value, 'sup', [(i, (i + steps) % n_sup) for i in range(n_sup)])  9.97 us
    all_to_all x2, starting transfers between devices, exchange(): lax.all_to_all(value, ('pair', 'head'), split_axis=0, concat_axis=0, tile...  8.66 us
    all_to_all x2, waiting for transfers between devices, exchange(): lax.all_to_all(value, ('pair', 'head'), split_axis=0, concat_axis=0, tile...  8.15 us
    pallas_call x1, Pallas kernels, pack_queries(): pl.pallas_call(kernel, out_shape=[jax.ShapeDtypeStruct((rows, HD), BF16)]...  5.54 us
    unnamed x28, local copies, waits for them, and re-layouts  4.21 us
  transfers between devices with their start and end apart: 20, of which 12 were waited for; matrix products, arithmetic and copies ran while one was open for 0% of the time, Pallas kernels for 29%

commit v1 on v0

--- a/solution.py
+++ b/solution.py
@@ -15,8 +15,6 @@
 F32 = jnp.float32
 BF16 = jnp.bfloat16
 EXTRA = 32
-UNROLL = 4
-PIPELINED = False
 VMEM_LIMIT = 16 * 1024 * 1024
 VMEM_ALL = 60 * 1024 * 1024
 
@@ -60,56 +58,57 @@
     return a, b, c
 
 
-def pack_queries(me, query, out_grad, forward_out, log_norm, parts):
+def pack_queries(me, query, out_grad, forward_out, log_norm, parts, offsets):
     tokens = query.shape[0]
     heads = log_norm.shape[0] // parts
     width = heads * HD
     rows = 2 * heads * tokens + EXTRA
+    count = len(offsets)
 
     def kernel(me_ref, q_ref, g_ref, f_ref, n_ref, *refs):
-        outs = refs[:parts]
-        q_buf, g_buf, f_buf, n_buf, sem, n_sem = refs[parts:]
+        outs = refs[:count]
+        q_buf, g_buf, f_buf, n_buf, sem, n_sem = refs[count:]
         n_load = pltpu.make_async_copy(n_ref, n_buf, n_sem)
         n_load.start()
         loads = []
-        for d in range(parts):
+        for s, d in enumerate(offsets):
             start = jnp.bitwise_xor(me_ref[0], d) * width
             lanes = pl.ds(pl.multiple_of(start, width), width)
             loads.append(
                 [
-                    pltpu.make_async_copy(ref.at[:, lanes], buf.at[d], sem.at[i, d])
+                    pltpu.make_async_copy(ref.at[:, lanes], buf.at[s], sem.at[i, s])
                     for i, (ref, buf) in enumerate(((g_ref, g_buf), (f_ref, f_buf), (q_ref, q_buf)))
                 ]
             )
-            for copy in loads[d]:
+            for copy in loads[s]:
                 copy.start()
         line = lax.broadcasted_iota(jnp.int32, (16, width), 0)
         lane = lax.broadcasted_iota(jnp.int32, (16, width), 1)
         pick = jnp.where(lane // HD == line, 1.0, 0.0).astype(BF16)
         pad = jnp.zeros((EXTRA - 6 * heads, tokens), BF16)
         n_load.wait()
-        for d, out in enumerate(outs):
-            for copy in loads[d]:
+        for s, (d, out) in enumerate(zip(offsets, outs)):
+            for copy in loads[s]:
                 copy.wait()
-            prod = g_buf[d].astype(F32) * f_buf[d].astype(F32)
+            prod = g_buf[s].astype(F32) * f_buf[s].astype(F32)
             high = prod.astype(BF16)
             low = (prod - high.astype(F32)).astype(BF16)
             delta = (dot(pick, high, ((1,), (1,))) + dot(pick, low, ((1,), (1,))))[:heads]
             norm = n_buf[jnp.bitwise_xor(me_ref[0], d)]
             for h in range(heads):
-                out[h * tokens : (h + 1) * tokens, :] = q_buf[d, :, h * HD : (h + 1) * HD]
-                out[(heads + h) * tokens : (heads + h + 1) * tokens, :] = g_buf[d, :, h * HD : (h + 1) * HD]
+                out[h * tokens : (h + 1) * tokens, :] = q_buf[s, :, h * HD : (h + 1) * HD]
+                out[(heads + h) * tokens : (heads + h + 1) * tokens, :] = g_buf[s, :, h * HD : (h + 1) * HD]
             out[2 * heads * tokens :, :] = jnp.concatenate(split3(norm) + split3(delta) + (pad,), axis=0)
 
     return pl.pallas_call(
         kernel,
-        out_shape=[jax.ShapeDtypeStruct((rows, HD), BF16)] * parts,
+        out_shape=[jax.ShapeDtypeStruct((rows, HD), BF16)] * count,
         in_specs=[SCALARS] + [ANYWHERE] * 4,
-        out_specs=[WHOLE] * parts,
-        scratch_shapes=[pltpu.VMEM((parts, tokens, width), BF16)] * 3
+        out_specs=[WHOLE] * count,
+        scratch_shapes=[pltpu.VMEM((count, tokens, width), BF16)] * 3
         + [
             pltpu.VMEM((parts, heads, tokens), F32),
-            pltpu.SemaphoreType.DMA((3, parts)),
+            pltpu.SemaphoreType.DMA((3, count)),
             pltpu.SemaphoreType.DMA,
         ],
         compiler_params=pltpu.CompilerParams(vmem_limit_bytes=VMEM_ALL),
@@ -121,7 +120,7 @@
     return jnp.concatenate([x[h : h + 1] for h in range(x.shape[0])], axis=1)
 
 
-def terms(where, masks, work, queries, kvs, dq_in, acc_in, dq_done, acc_done, tiles, heads):
+def terms(where, masks, work, queries, kvs, dq_in, acc_in, dq_done, acc_done, unroll, tiles, heads):
     shards_in = [d for d, _ in work]
     names = [n for n in ("own", "one", "two") if any(n in use for _, use in work)]
     tokens = (queries[shards_in[0]].shape[0] - EXTRA) // (2 * heads)
@@ -138,25 +137,21 @@
     starts = {n: sum(sizes[m] for m in names[:i]) for i, n in enumerate(names)}
     total = sum(sizes.values())
     acc_shapes = [jax.ShapeDtypeStruct((sizes[n], tokens, 2 * HD), BF16 if n in acc_done else F32) for n in names]
-    longest = sum(2 * tiles * len(use) + UNROLL for _, use in work) + 4 * UNROLL
-    block = UNROLL * tokens
+    longest = sum(2 * tiles * len(use) + unroll for _, use in work) + unroll
     scratch = [
         pltpu.VMEM((len(work), 2 * rows, HD), BF16),
         pltpu.VMEM((len(work), 2, rows), F32),
         pltpu.VMEM((total, 2 * tokens, HD), BF16),
         pltpu.VMEM((total, tokens, 2 * HD), F32),
         pltpu.VMEM((len(work), HD, rows), F32),
-        pltpu.SMEM((longest,), jnp.int32),
-        pltpu.SMEM((longest,), F32),
-        pltpu.SMEM((longest,), jnp.int32),
-    ] + [pltpu.VMEM((block, rows), F32)] * (4 if PIPELINED else 0)
+    ] + [pltpu.SMEM((longest,), jnp.int32)] * 3
 
     def kernel(where_ref, mask_ref, *refs):
         refs = list(refs)
         take = lambda keys: {k: refs.pop(0) for k in keys}
         q_refs, kv_refs, dq_old, acc_old = take(shards_in), take(names), take(dq_given), take(acc_given)
         dq_out, acc_out = take(shards_in), take(names)
-        q_buf, line_buf, kv_buf, acc, dq_acc, todo, penalty, shard_of = refs[:8]
+        q_buf, line_buf, kv_buf, acc, dq_acc, todo, shard_of, end_of = refs
         pair, head = where_ref[0], where_ref[1]
         for n in names:
             here = pl.ds(starts[n], sizes[n])
@@ -190,73 +185,39 @@
             begin = place
             for tile, flag in wanted:
                 todo[place] = jnp.int32(tile)
-                penalty[place] = 0.0
                 place = place + flag
-            for u in range(UNROLL - 1):
+            for u in range(unroll - 1):
                 todo[place + u] = jnp.int32(0)
-                penalty[place + u] = 1e30
-            place = begin + (place - begin + UNROLL - 1) // UNROLL * UNROLL
-            for g in range((len(wanted) + UNROLL - 1) // UNROLL):
-                shard_of[begin // UNROLL + g] = jnp.int32(slot)
-        groups = place // UNROLL
-        for u in range(2 * UNROLL):
-            todo[place + u] = jnp.int32(0)
-            penalty[place + u] = 1e30
-        shard_of[groups] = jnp.int32(0)
-        shard_of[groups + 1] = jnp.int32(0)
-
-        def load(g):
+            for g in range((len(wanted) + unroll - 1) // unroll):
+                shard_of[begin // unroll + g] = jnp.int32(slot)
+                end_of[begin // unroll + g] = place
+            place = begin + (place - begin + unroll - 1) // unroll * unroll
+
+        def body(g, carry):
             slot = shard_of[g]
-            spots = [todo[g * UNROLL + u] for u in range(UNROLL)]
+            spots = [todo[g * unroll + u] for u in range(unroll)]
+            q, grad = q_buf[slot, :rows, :], q_buf[slot, rows:, :]
             k = jnp.concatenate([kv_buf[t, :tokens, :] for t in spots], axis=0)
-            return slot, spots, k
-
-        def before(g):
-            slot, spots, k = load(g)
             v = jnp.concatenate([kv_buf[t, tokens:, :] for t in spots], axis=0)
-            return dot(k, q_buf[slot, :rows, :], ((1,), (1,))), dot(v, q_buf[slot, rows:, :], ((1,), (1,)))
-
-        def after(g, score, dprob):
-            slot, spots, k = load(g)
             lines = line_buf[slot]
-            prob = jnp.concatenate(
-                [
-                    jnp.exp2(
-                        score[u * tokens : (u + 1) * tokens] * (SCALE * LOG2E)
-                        - (lines[0:1] + penalty[g * UNROLL + u])
-                    )
-                    for u in range(UNROLL)
-                ],
-                axis=0,
-            )
+            score = dot(k, q, ((1,), (1,)))
+            dprob = dot(v, grad, ((1,), (1,)))
+            prob = []
+            for u in range(unroll):
+                nothing = jnp.where(g * unroll + u < end_of[g], jnp.float32(0.0), jnp.float32(1e30))
+                part = score[u * tokens : (u + 1) * tokens] * (SCALE * LOG2E)
+                prob.append(jnp.exp2(part - (lines[0:1] + nothing)))
+            prob = jnp.concatenate(prob, axis=0)
             dscore = (prob * (dprob - lines[1:2])).astype(BF16)
-            dv = dot(prob.astype(BF16), q_buf[slot, rows:, :], ((1,), (0,)))
-            dk = dot(dscore, q_buf[slot, :rows, :], ((1,), (0,)))
+            dv = dot(prob.astype(BF16), grad, ((1,), (0,)))
+            dk = dot(dscore, q, ((1,), (0,)))
             dq_acc[slot] += dot(k, dscore, ((0,), (0,)))
             for u, t in enumerate(spots):
                 acc[t, :, :HD] += dk[u * tokens : (u + 1) * tokens]
                 acc[t, :, HD:] += dv[u * tokens : (u + 1) * tokens]
-
-        if PIPELINED:
-            s0, p0, s1, p1 = refs[8:]
-            s0[...], p0[...] = before(0)
-
-            def body(i, carry):
-                g = 2 * i
-                s1[...], p1[...] = before(g + 1)
-                after(g, s0[...], p0[...])
-                s0[...], p0[...] = before(g + 2)
-                after(g + 1, s1[...], p1[...])
-                return carry
-
-            lax.fori_loop(0, (groups + 1) // 2, body, 0)
-        else:
-
-            def body(g, carry):
-                after(g, *before(g))
-                return carry
-
-            lax.fori_loop(0, groups, body, 0)
+            return carry
+
+        lax.fori_loop(0, place // unroll, body, 0)
 
         for slot, d in enumerate(shards_in):
             if d in dq_done:
@@ -283,25 +244,11 @@
     return dict(zip(shards_in, outs)), dict(zip(names, outs[len(shards_in) :]))
 
 
-def total_kv(own, one, two, after):
-    tiles = two.shape[0]
-
-    def kernel(own_ref, one_ref, two_ref, *refs):
-        out_ref = refs[-1]
-        for t in range(2 * tiles):
-            total = own_ref[t] + one_ref[t].astype(F32)
-            if t >= tiles:
-                total = total + two_ref[t - tiles].astype(F32)
-            out_ref[t, :, :HD] = (total[:, :HD] * SCALE).astype(BF16)
-            out_ref[t, :, HD:] = total[:, HD:].astype(BF16)
-
-    return pl.pallas_call(
-        kernel,
-        out_shape=jax.ShapeDtypeStruct(own.shape, BF16),
-        in_specs=[WHOLE] * 3 + [ANYWHERE] * len(after),
-        out_specs=WHOLE,
-        name="total_kv",
-    )(own, one, two, *after)
+def total_kv(own, one, two):
+    lane = lax.broadcasted_iota(jnp.int32, (1, 1, 2 * HD), 2)
+    lower = jnp.zeros_like(two)
+    total = own + one.astype(F32) + jnp.concatenate([lower, two], axis=0).astype(F32)
+    return (total * jnp.where(lane < HD, F32(SCALE), F32(1.0))).astype(BF16)
 
 
 def unpack_queries(me, grads, tokens):
@@ -327,19 +274,8 @@
 
 def unpack_kv(grads):
     parts, tokens = grads.shape[:2]
-
-    def kernel(in_ref, k_ref, v_ref):
-        for g in range(parts):
-            k_ref[:, g * HD : (g + 1) * HD] = in_ref[g, :, :HD]
-            v_ref[:, g * HD : (g + 1) * HD] = in_ref[g, :, HD:]
-
-    return pl.pallas_call(
-        kernel,
-        out_shape=[jax.ShapeDtypeStruct((tokens, parts * HD), BF16)] * 2,
-        in_specs=[WHOLE],
-        out_specs=[WHOLE] * 2,
-        name="unpack_kv",
-    )(grads)
+    lines = lambda x: x.transpose(1, 0, 2).reshape(tokens, parts * HD)
+    return lines(grads[:, :, :HD]), lines(grads[:, :, HD:])
 
 
 def shards(sizes, query, keys, values, forward_out, out_grad, log_norm, tile_mask):
@@ -366,32 +302,35 @@
         return lax.all_to_all(value, ("pair", "head"), split_axis=0, concat_axis=0, tiled=True)
 
     kv_own = exchange(pack_kv(keys, values, tile_mask, parts))
-    packed = pack_queries(me, query, out_grad, forward_out, log_norm, parts)
     first = [0, 1, 2, n_head]
     last = [parts - 2, parts - 1]
     middle = [d for d in range(parts) if d not in first + last]
-    queries = {d: swap(packed[d], d) if d else packed[d] for d in first}
-    held, kv_own = lax.optimization_barrier(([packed[d] for d in middle], kv_own))
+    packed = {}
+    for some in (first + middle, [d for d in range(parts) if d not in first + middle]):
+        packed.update(zip(some, pack_queries(me, query, out_grad, forward_out, log_norm, parts, some)))
+    queries = {d: swap(packed[d], d) if d else packed[d] for d in first + middle}
+    queries[1], kv_own = lax.optimization_barrier((queries[1], kv_own))
     kvs = {"own": kv_own, "one": along(kv_own, 1), "two": along(kv_own[n_head:], 2)}
-    queries.update({d: swap(x, d) for d, x in zip(middle, held)})
     held, arrived = lax.optimization_barrier(([packed[d] for d in last], [queries[d] for d in first[2:]]))
     queries.update(dict(zip(first[2:], arrived)))
     queries.update({d: swap(x, d) for d, x in zip(last, held)})
     masks = kv_own[::n_head, 2 * tokens :, :tiles].astype(jnp.int32).reshape(n_pair, -1)
     args = dict(tiles=tiles, heads=heads)
-    call = lambda work, dq, acc, dq_done, acc_done: terms(
-        where, masks, work, queries, kvs, dq, acc, dq_done, acc_done, **args
+    call = lambda work, dq, acc, dq_done, acc_done, unroll=4: terms(
+        where, masks, work, queries, kvs, dq, acc, dq_done, acc_done, unroll, **args
     )
+    rest = middle + last
     dq, sums = call([(d, ["own"]) for d in first], {}, {}, [], [])
-    some, sums = call([(d, ["one"]) for d in first] + [(d, ["own", "one"]) for d in middle], dq, sums, [], [])
-    dq.update(some)
-    some, sums = call([(d, ["own", "one"]) for d in last], {}, sums, [], ["one"])
+    dq, one = call([(d, ["one"]) for d in first], dq, {}, [], [])
+    sums.update(one)
+    some, sums = call([(d, ["own", "one"]) for d in rest], {}, sums, [], ["one"])
     dq.update(some)
     one = along(sums["one"], -1)
-    grads, two = call([(d, ["two"]) for d in range(parts)], dq, {}, list(range(parts)), ["two"])
+    grads, two = call([(d, ["two"]) for d in range(parts)], dq, {}, list(range(parts)), ["two"], 2)
     two = along(two["two"], -2)
     grads = [swap(grads[d], d) if d else grads[d] for d in range(parts)]
-    kv_grad = exchange(total_kv(sums["own"], one, two, grads[1:]))
+    one, two, grads[1:] = lax.optimization_barrier((one, two, grads[1:]))
+    kv_grad = exchange(total_kv(sums["own"], one, two))
     query_grad = unpack_queries(me, grads, tokens)
     keys_grad, values_grad = unpack_kv(kv_grad)
     return query_grad, keys_grad, values_grad

time: 104 us -> 93.7 us (0.901); the launches traced: 102 us -> 93 us
  starting transfers between devices: 32.7 us -> 27.5 us
  Pallas kernels: 36 us -> 32.8 us
  waiting for transfers between devices: 28.4 us -> 26.9 us
    pallas_call x2 -> x0, Pallas kernels: 4.34 us -> none  [the longest x1 2.36 us: total_kv(): pl.pallas_call(kernel, out_shape=jax.ShapeDtypeStruct(own.shape, BF16), i...]
    ppermute x14, waiting for transfers between devices: 19.3 us -> 16.1 us  [swap(): return lax.ppermute(value, ('head', 'pair'), pairs)]
    ppermute x14, starting transfers between devices: 14 us -> 11.2 us  [swap(): return lax.ppermute(value, ('head', 'pair'), pairs)]
    ppermute x4, starting transfers between devices: 9.97 us -> 7.6 us  [along(): lax.ppermute(value, 'sup', [(i, (i + steps) % n_sup) for i in range(n_sup)])]
    unnamed x28 -> x22, local copies, waits for them, and re-layouts: 4.21 us -> 2.63 us
    all_to_all x2, waiting for transfers between devices: 8.15 us -> 9.58 us  [exchange(): lax.all_to_all(value, ('pair', 'head'), split_axis=0, concat_axis=0, tile...]
    pallas_call x1 -> x2, Pallas kernels: 5.54 us -> 6.78 us  [pack_queries(): pl.pallas_call(kernel, out_shape=[jax.ShapeDtypeStruct((rows, HD), BF16)]...]
  transfers between devices with their start and end apart: 20 -> 20, of which waited for: 12 -> 12; matrix products, arithmetic and copies ran while one was open for 0% -> 1% of each run, Pallas kernels for 29% -> 33%
where the time goes in v1:
time: 93.7 us; the launch traced here: 93 us
  Pallas kernels  32.8 us (35%)
  starting transfers between devices  27.5 us (29%)
  waiting for transfers between devices  26.9 us (29%)
  local copies, waits for them, and re-layouts  3.92 us (4%)
  other arithmetic  1.05 us (1%)
    pallas_call x4, Pallas kernels, terms(): pl.pallas_call(kernel, out_shape=dq_shapes + acc_shapes, in_specs=[SCALAR...  21.6 us
    ppermute x14, waiting for transfers between devices, swap(): return lax.ppermute(value, ('head', 'pair'), pairs)  16.1 us
    ppermute x14, starting transfers between devices, swap(): return lax.ppermute(value, ('head', 'pair'), pairs)  11.2 us
    all_to_all x2, waiting for transfers between devices, exchange(): lax.all_to_all(value, ('pair', 'head'), split_axis=0, concat_axis=0, tile...  9.58 us
    all_to_all x2, starting transfers between devices, exchange(): lax.all_to_all(value, ('pair', 'head'), split_axis=0, concat_axis=0, tile...  8.67 us
    ppermute x4, starting transfers between devices, along(): lax.ppermute(value, 'sup', [(i, (i + steps) % n_sup) for i in range(n_sup)])  7.6 us
    pallas_call x2, Pallas kernels, pack_queries(): pl.pallas_call(kernel, out_shape=[jax.ShapeDtypeStruct((rows, HD), BF16)]...  6.78 us
    unnamed x22, local copies, waits for them, and re-layouts  2.63 us
  transfers between devices with their start and end apart: 20, of which 12 were waited for; matrix products, arithmetic and copies ran while one was open for 1% of the time, Pallas kernels for 33%

profile of v1, /device:TPU:0, one launch (start us, length us, event | category | flops | bytes accessed | tf_op | source)
XLA Modules:
  0.0 93.0 jit_solution(7565147010389007540)
XLA Ops:
  0.6 1.9 %pack_kv.1 = bf16[8,272,128]{2,1,0:T(8,128)(2,1)} custom-call(bf16[128,1024]{1,0:T(8,128)(2,1)} %k_ref.1, bf16[128,1024]{1,0:T(8,128)(2,1)} %v_ref.1, s32[1,4,4,4]{3,2,1,0:T(4,128)} %m_ref.1), custom_call_target="tpu_custom_call" | custom-call | tf_op jit(solution)/shard_map/pack_kv/pallas_call | solution.py:43
  2.6 5.2 %all-to-all-start = ((bf16[8,272,128]{2,1,0:T(8,128)(2,1)}), bf16[8,272,128]{2,1,0:T(8,128)(2,1)S(1)}, u32[]{:S(2)}, u32[]{:S(2)}) async-start(bf16[8,272,128]{2,1,0:T(8,128)(2,1)} %pack_kv.1), calls=%async_computation | async-start | bytes 1114112 | tf_op jit(solution)/shard_map/all_to_all | solution.py:302
  7.7 4.4 %pack_queries.2 = (bf16[1056,128]{1,0:T(8,128)(2,1)}, bf16[1056,128]{1,0:T(8,128)(2,1)}, bf16[1056,128]{1,0:T(8,128)(2,1)}, bf16[1056,128]{1,0:T(8,128)(2,1)}, b...) custom-call(s32[1]{0:T(128)} %bitcast.me_ref, bf16[128,4096]{1,0:T(8,128)(2,1)} %q_ref.3, bf16[128,4096]{1,0:T(8,128)(2,1)} %g_ref.3, ...), custom_call_target="tpu_custom_call" | custom-call | tf_op jit(solution)/shard_map/pack_queries/pallas_call | solution.py:103
  12.7 1.7 %collective-permute-start.1 = (bf16[1056,128]{1,0:T(8,128)(2,1)}, bf16[1056,128]{1,0:T(8,128)(2,1)S(1)}, u32[]{:S(2)}, u32[]{:S(2)}) collective-permute-start(bf16[1056,128]{1,0:T(8,128)(2,1)} %get-tuple-element.57), channel_id=1, source_target_pairs={{0,16},{1,17},{8,24},{9,25},{16,0},{17,1},{24,8},{25,9},{2,18},{3,... | collective-permute-start | bytes 811016 | tf_op jit(solution)/shard_map/ppermute | solution.py:296
  14.4 1.5 %collective-permute-start.2 = (bf16[1056,128]{1,0:T(8,128)(2,1)}, bf16[1056,128]{1,0:T(8,128)(2,1)S(1)}, u32[]{:S(2)}, u32[]{:S(2)}) collective-permute-start(bf16[1056,128]{1,0:T(8,128)(2,1)} %get-tuple-element.58), channel_id=1, source_target_pairs={{0,1},{1,0},{8,9},{9,8},{16,17},{17,16},{24,25},{25,24},{2,3},{3,2... | collective-permute-start | bytes 811016 | tf_op jit(solution)/shard_map/ppermute | solution.py:296
  15.9 2.4 %all-to-all-done.refs_4_ = bf16[8,272,128]{2,1,0:T(8,128)(2,1)S(1)} async-done(((bf16[8,272,128]{2,1,0:T(8,128)(2,1)}), bf16[8,272,128]{2,1,0:T(8,128)(2,1)S(1)}, u32[]{:S(2)}, u32[]{:S(2)}) %all-to-all-start) | async-done | bytes 557088 | tf_op jit(solution)/shard_map/all_to_all | solution.py:302
  18.3 1.6 %collective-permute-start.8 = (bf16[8,272,128]{2,1,0:T(8,128)(2,1)S(1)}, bf16[8,272,128]{2,1,0:T(8,128)(2,1)S(1)}, u32[]{:S(2)}, u32[]{:S(2)}) collective-permute-start(bf16[8,272,128]{2,1,0:T(8,128)(2,1)S(1)} %all-to-all-done.refs_4_), channel_id=1, source_target_pairs={{0,2},{2,4},{4,6},{6,0},{1,3},{3,5},{5,7},{7,1},{8,10},{10,12},{12... | collective-permute-start | bytes 1671176 | tf_op jit(solution)/shard_map/ppermute | solution.py:299
  20.3 2.4 %pack_queries.3 = (bf16[1056,128]{1,0:T(8,128)(2,1)}, bf16[1056,128]{1,0:T(8,128)(2,1)}) custom-call(s32[1]{0:T(128)} %bitcast.me_ref, bf16[128,4096]{1,0:T(8,128)(2,1)} %q_ref.3, bf16[128,4096]{1,0:T(8,128)(2,1)} %g_ref.3, bf16[128,4096]{1,0:T(8,128)(2,1)} %f_ref.3, f32[8,4,128]{2,1,0:T(4,128)} %bitcast.13), custom_call_target="tpu_custom_call" | custom-call | tf_op jit(solution)/shard_map/pack_queries/pallas_call | solution.py:103
  22.7 1.3 %collective-permute-done.2.refs_3_.refs_4_ = bf16[1056,128]{1,0:T(8,128)(2,1)S(1)} collective-permute-done((bf16[1056,128]{1,0:T(8,128)(2,1)}, bf16[1056,128]{1,0:T(8,128)(2,1)S(1)}, u32[]{:S(2)}, u32[]{:S(2)}) %collective-permute-start.2) | collective-permute-done | bytes 270368 | tf_op jit(solution)/shard_map/ppermute | solution.py:296
  24.0 1.6 %collective-permute-start.5 = (bf16[1056,128]{1,0:T(8,128)(2,1)}, bf16[1056,128]{1,0:T(8,128)(2,1)S(1)}, u32[]{:S(2)}, u32[]{:S(2)}) collective-permute-start(bf16[1056,128]{1,0:T(8,128)(2,1)} %get-tuple-element.63), channel_id=1, source_target_pairs={{0,17},{1,16},{8,25},{9,24},{16,1},{17,0},{24,9},{25,8},{2,19},{3,... | collective-permute-start | bytes 811016 | tf_op jit(solution)/shard_map/ppermute | solution.py:296
  26.7 4.2 %terms.4 = (f32[128,512]{1,0:T(8,128)S(1)}, f32[128,512]{1,0:T(8,128)S(1)}, f32[128,512]{1,0:T(8,128)S(1)}, f32[128,512]{1,0:T(8,128)S(1)}, f32[8,128,256]{2,1,0:T(8,128)S(1)}) custom-call(s32[2]{0:T(128)S(1)} %pad_add_fusion.where_ref, s32[2,64]{1,0:T(2,128)S(1)} %reshape.38.mask_ref, bf16[1056,128]{1,0:T(8,128)(2,1)S(1)} %copy-done.1, ...), custom_call_target="tpu_custom_call" | custom-call | flops 1342177280 | bytes 1638400 | tf_op jit(solution)/shard_map/terms/pallas_call | solution.py:230
  30.9 1.2 %collective-permute-done.8.refs_4_.refs_5_ = bf16[8,272,128]{2,1,0:T(8,128)(2,1)S(1)} collective-permute-done((bf16[8,272,128]{2,1,0:T(8,128)(2,1)S(1)}, bf16[8,272,128]{2,1,0:T(8,128)(2,1)S(1)}, u32[]{:S(2)}, u32[]{:S(2)}) %collective-permute-start.8) | collective-permute-done | bytes 557088 | tf_op jit(solution)/shard_map/ppermute | solution.py:299
  32.1 1.5 %collective-permute-start.7 = (bf16[4,272,128]{2,1,0:T(8,128)(2,1)S(1)}, bf16[4,272,128]{2,1,0:T(8,128)(2,1)S(1)}, u32[]{:S(2)}, u32[]{:S(2)}) collective-permute-start(bf16[4,272,128]{2,1,0:T(8,128)(2,1)S(1)} %copy-done.2), channel_id=1, source_target_pairs={{0,4},{2,6},{4,0},{6,2},{1,5},{3,7},{5,1},{7,3},{8,12},{10,14},{12... | collective-permute-start | bytes 835592 | tf_op jit(solution)/shard_map/ppermute | solution.py:299
  33.5 5.0 %terms.5 = (f32[128,512]{1,0:T(8,128)S(1)}, f32[128,512]{1,0:T(8,128)S(1)}, f32[128,512]{1,0:T(8,128)S(1)}, f32[128,512]{1,0:T(8,128)S(1)}, f32[8,128,256]{2,1,0:T(8,128)S(1)}) custom-call(s32[2]{0:T(128)S(1)} %pad_add_fusion.where_ref, s32[2,64]{1,0:T(2,128)S(1)} %reshape.38.mask_ref, bf16[1056,128]{1,0:T(8,128)(2,1)S(1)} %copy-done.1, ...), custom_call_target="tpu_custom_call" | custom-call | flops 1342177280 | bytes 2162688 | tf_op jit(solution)/shard_map/terms/pallas_call | solution.py:230
  38.5 1.1 %collective-permute-done.4.refs_1_.refs_5_ = bf16[1056,128]{1,0:T(8,128)(2,1)S(1)} collective-permute-done((bf16[1056,128]{1,0:T(8,128)(2,1)}, bf16[1056,128]{1,0:T(8,128)(2,1)S(1)}, u32[]{:S(2)}, u32[]{:S(2)}) %collective-permute-start.4) | collective-permute-done | bytes 270368 | tf_op jit(solution)/shard_map/ppermute | solution.py:296
  39.6 0.9 collective-permute-done.6.refs_3_.refs_7_
  40.5 8.3 %terms.6 = (f32[128,512]{1,0:T(8,128)S(1)}, f32[128,512]{1,0:T(8,128)S(1)}, f32[128,512]{1,0:T(8,128)S(1)}, f32[128,512]{1,0:T(8,128)S(1)}, f32[8,128,256]{2,1,0...) custom-call(s32[2]{0:T(128)S(1)} %pad_add_fusion.where_ref, s32[2,64]{1,0:T(2,128)S(1)} %reshape.38.mask_ref, ...), custom_call_target="tpu_custom_call" | custom-call | flops 2684354560 | bytes 3244032 | tf_op jit(solution)/shard_map/terms/pallas_call | solution.py:230
  48.9 4.5 %collective-permute-start.9 = (bf16[8,128,256]{2,1,0:T(8,128)(2,1)S(1)}, bf16[8,128,256]{2,1,0:T(8,128)(2,1)S(1)}, u32[]{:S(2)}, u32[]{:S(2)}) collective-permute-start(bf16[8,128,256]{2,1,0:T(8,128)(2,1)S(1)} %get-tuple-element.80), channel_id=1, source_target_pairs={{0,6},{2,0},{4,2},{6,4},{1,7},{3,1},{5,3},{7,5},{8,14},{10,8},{12,... | collective-permute-start | bytes 1572872 | tf_op jit(solution)/shard_map/ppermute | solution.py:299
  53.3 4.1 %terms.7 = (bf16[512,128]{1,0:T(8,128)(2,1)S(1)}, bf16[512,128]{1,0:T(8,128)(2,1)S(1)}, bf16[512,128]{1,0:T(8,128)(2,1)S(1)}, bf16[512,128]{1,0:T(8,128)(2,1)S(1...) custom-call(s32[2]{0:T(128)S(1)} %pad_add_fusion.where_ref, ...), custom_call_target="tpu_custom_call" | custom-call | flops 2684354560 | bytes 3489792 | tf_op jit(solution)/shard_map/terms/pallas_call | solution.py:230
  58.1 1.1 %collective-permute-start.11 = (bf16[512,128]{1,0:T(8,128)(2,1)S(1)}, bf16[512,128]{1,0:T(8,128)(2,1)S(1)}, u32[]{:S(2)}, u32[]{:S(2)}) collective-permute-start(bf16[512,128]{1,0:T(8,128)(2,1)S(1)} %get-tuple-element.82), channel_id=1, source_target_pairs={{0,8},{1,9},{8,0},{9,1},{16,24},{17,25},{24,16},{25,17},{2,10},{3,... | collective-permute-start | bytes 393224 | tf_op jit(solution)/shard_map/ppermute | solution.py:296
  59.2 1.4 %collective-permute-start.13 = (bf16[512,128]{1,0:T(8,128)(2,1)S(1)}, bf16[512,128]{1,0:T(8,128)(2,1)S(1)}, u32[]{:S(2)}, u32[]{:S(2)}) collective-permute-start(bf16[512,128]{1,0:T(8,128)(2,1)S(1)} %get-tuple-element.84), channel_id=1, source_target_pairs={{0,24},{1,25},{8,16},{9,17},{16,8},{17,9},{24,0},{25,1},{2,26},{3,... | collective-permute-start | bytes 393224 | tf_op jit(solution)/shard_map/ppermute | solution.py:296
  60.7 4.9 %collective-permute-done.12.refs_2_ = bf16[512,128]{1,0:T(8,128)(2,1)S(1)} collective-permute-done((bf16[512,128]{1,0:T(8,128)(2,1)S(1)}, bf16[512,128]{1,0:T(8,128)(2,1)S(1)}, u32[]{:S(2)}, u32[]{:S(2)}) %collective-permute-start.12) | collective-permute-done | bytes 131104 | tf_op jit(solution)/shard_map/ppermute | solution.py:296
  65.6 0.9 collective-permute-done.13.refs_3_
  66.8 3.0 %collective-permute-start.17 = (bf16[512,128]{1,0:T(8,128)(2,1)S(1)}, bf16[512,128]{1,0:T(8,128)(2,1)S(1)}, u32[]{:S(2)}, u32[]{:S(2)}) collective-permute-start(bf16[512,128]{1,0:T(8,128)(2,1)S(1)} %get-tuple-element.88), channel_id=1, source_target_pairs={{0,25},{1,24},{8,17},{9,16},{16,9},{17,8},{24,1},{25,0},{2,27},{3,... | collective-permute-start | bytes 393224 | tf_op jit(solution)/shard_map/ppermute | solution.py:296
  70.0 3.6 %collective-permute-done.16.refs_6_ = bf16[512,128]{1,0:T(8,128)(2,1)S(1)} collective-permute-done((bf16[512,128]{1,0:T(8,128)(2,1)S(1)}, bf16[512,128]{1,0:T(8,128)(2,1)S(1)}, u32[]{:S(2)}, u32[]{:S(2)}) %collective-permute-start.16) | collective-permute-done | bytes 131104 | tf_op jit(solution)/shard_map/ppermute | solution.py:296
  73.6 2.9 %collective-permute-done.17.refs_7_ = bf16[512,128]{1,0:T(8,128)(2,1)S(1)} collective-permute-done((bf16[512,128]{1,0:T(8,128)(2,1)S(1)}, bf16[512,128]{1,0:T(8,128)(2,1)S(1)}, u32[]{:S(2)}, u32[]{:S(2)}) %collective-permute-start.17) | collective-permute-done | bytes 131104 | tf_op jit(solution)/shard_map/ppermute | solution.py:296
  76.6 1.0 %multiply_convert_fusion = bf16[8,128,256]{2,1,0:T(8,128)(2,1)} fusion(f32[8,128,256]{2,1,0:T(8,128)S(1)} %get-tuple-element.96, bf16[8,128,256]{2,1,0:T(8,128)(2,1)S(1)} %collective-permute-done.9, f32[256]{0:T(256)S(1)} %compare_select_fusion, bf16[4,128,256]{2,1,0:T(8,128)(2,1)S(1)} %collective-permute-done.10), kind=kLoop, calls=%fused_computation | loop fusion | flops 1572864 | bytes 2360320 | tf_op jit(solution)/shard_map/convert_element_type | solution.py:251
  77.6 3.5 %all-to-all-start.1 = ((bf16[8,128,256]{2,1,0:T(8,128)(2,1)}), bf16[8,128,256]{2,1,0:T(8,128)(2,1)S(1)}, u32[]{:S(2)}, u32[]{:S(2)}) async-start(bf16[8,128,256]{2,1,0:T(8,128)(2,1)} %multiply_convert_fusion), calls=%async_computation.1 | async-start | bytes 1048576 | tf_op jit(solution)/shard_map/all_to_all | solution.py:302
  81.1 2.5 %unpack_queries.1 = bf16[128,4096]{1,0:T(8,128)(2,1)} custom-call(s32[1]{0:T(128)} %bitcast.me_ref, bf16[512,128]{1,0:T(8,128)(2,1)} %copy-done, bf16[512,128]{1,0:T(8,128)(2,1)} %copy-done.3, bf16[512,128]{1,0:T(8,128)(2,1)} %copy-done.4, bf16[512,128]{1,0:T(8,128)(2,1)} %copy-done.5, bf16[512,128]{1,0:T(8,128)(2,1)} %copy-done.6, ...), custom_call_target="tpu_custom_call" | custom-call | tf_op jit(solution)/shard_map/unpack_queries/pallas_call | solution.py:266
  83.6 7.1 %all-to-all-done.1 = bf16[8,128,256]{2,1,0:T(8,128)(2,1)S(1)} async-done(((bf16[8,128,256]{2,1,0:T(8,128)(2,1)}), bf16[8,128,256]{2,1,0:T(8,128)(2,1)S(1)}, u32[]{:S(2)}, u32[]{:S(2)}) %all-to-all-start.1) | async-done | bytes 524320 | tf_op jit(solution)/shard_map/all_to_all | solution.py:302
  91.1 0.9 copy.12
  92.1 0.9 copy.13
  (47 shorter events, 3.8 us)
Async XLA Ops:
  2.6 15.7 %all-to-all-start = ((bf16[8,272,128]{2,1,0:T(8,128)(2,1)}), bf16[8,272,128]{2,1,0:T(8,128)(2,1)S(1)}, u32[]{:S(2)}, u32[]{:S(2)}) async-start(bf16[8,272,128]{2,1,0:T(8,128)(2,1)} %pack_kv.1), calls=%async_computation | async-start | bytes 1114112 | tf_op jit(solution)/shard_map/all_to_all | solution.py:302
  12.1 3.7 %collective-permute-start = (bf16[1056,128]{1,0:T(8,128)(2,1)}, bf16[1056,128]{1,0:T(8,128)(2,1)S(1)}, u32[]{:S(2)}, u32[]{:S(2)}) collective-permute-start(bf16[1056,128]{1,0:T(8,128)(2,1)} %get-tuple-element.51), channel_id=1, source_target_pairs={{0,8},{1,9},{8,0},{9,1},{16,24},{17,25},{24,16},{25,17},{2,10},{3,... | collective-permute-start | bytes 811016 | tf_op jit(solution)/shard_map/ppermute | solution.py:296
  12.7 10.0 %collective-permute-start.1 = (bf16[1056,128]{1,0:T(8,128)(2,1)}, bf16[1056,128]{1,0:T(8,128)(2,1)S(1)}, u32[]{:S(2)}, u32[]{:S(2)}) collective-permute-start(bf16[1056,128]{1,0:T(8,128)(2,1)} %get-tuple-element.57), channel_id=1, source_target_pairs={{0,16},{1,17},{8,24},{9,25},{16,0},{17,1},{24,8},{25,9},{2,18},{3,... | collective-permute-start | bytes 811016 | tf_op jit(solution)/shard_map/ppermute | solution.py:296
  14.4 9.6 %collective-permute-start.2 = (bf16[1056,128]{1,0:T(8,128)(2,1)}, bf16[1056,128]{1,0:T(8,128)(2,1)S(1)}, u32[]{:S(2)}, u32[]{:S(2)}) collective-permute-start(bf16[1056,128]{1,0:T(8,128)(2,1)} %get-tuple-element.58), channel_id=1, source_target_pairs={{0,1},{1,0},{8,9},{9,8},{16,17},{17,16},{24,25},{25,24},{2,3},{3,2... | collective-permute-start | bytes 811016 | tf_op jit(solution)/shard_map/ppermute | solution.py:296
  18.3 13.7 %collective-permute-start.8 = (bf16[8,272,128]{2,1,0:T(8,128)(2,1)S(1)}, bf16[8,272,128]{2,1,0:T(8,128)(2,1)S(1)}, u32[]{:S(2)}, u32[]{:S(2)}) collective-permute-start(bf16[8,272,128]{2,1,0:T(8,128)(2,1)S(1)} %all-to-all-done.refs_4_), channel_id=1, source_target_pairs={{0,2},{2,4},{4,6},{6,0},{1,3},{3,5},{5,7},{7,1},{8,10},{10,12},{12... | collective-permute-start | bytes 1671176 | tf_op jit(solution)/shard_map/ppermute | solution.py:299
  19.9 18.6 %collective-permute-start.3 = (bf16[1056,128]{1,0:T(8,128)(2,1)}, bf16[1056,128]{1,0:T(8,128)(2,1)S(1)}, u32[]{:S(2)}, u32[]{:S(2)}) collective-permute-start(bf16[1056,128]{1,0:T(8,128)(2,1)} %get-tuple-element.60), channel_id=1, source_target_pairs={{0,24},{1,25},{8,16},{9,17},{16,8},{17,9},{24,0},{25,1},{2,26},{3,... | collective-permute-start | bytes 811016 | tf_op jit(solution)/shard_map/ppermute | solution.py:296
  19.9 19.7 %collective-permute-start.4 = (bf16[1056,128]{1,0:T(8,128)(2,1)}, bf16[1056,128]{1,0:T(8,128)(2,1)S(1)}, u32[]{:S(2)}, u32[]{:S(2)}) collective-permute-start(bf16[1056,128]{1,0:T(8,128)(2,1)} %get-tuple-element.62), channel_id=1, source_target_pairs={{0,9},{1,8},{8,1},{9,0},{16,25},{17,24},{24,17},{25,16},{2,11},{3,... | collective-permute-start | bytes 811016 | tf_op jit(solution)/shard_map/ppermute | solution.py:296
  24.0 15.6 %collective-permute-start.5 = (bf16[1056,128]{1,0:T(8,128)(2,1)}, bf16[1056,128]{1,0:T(8,128)(2,1)S(1)}, u32[]{:S(2)}, u32[]{:S(2)}) collective-permute-start(bf16[1056,128]{1,0:T(8,128)(2,1)} %get-tuple-element.63), channel_id=1, source_target_pairs={{0,17},{1,16},{8,25},{9,24},{16,1},{17,0},{24,9},{25,8},{2,19},{3,... | collective-permute-start | bytes 811016 | tf_op jit(solution)/shard_map/ppermute | solution.py:296
  25.6 14.9 %collective-permute-start.6 = (bf16[1056,128]{1,0:T(8,128)(2,1)}, bf16[1056,128]{1,0:T(8,128)(2,1)S(1)}, u32[]{:S(2)}, u32[]{:S(2)}) collective-permute-start(bf16[1056,128]{1,0:T(8,128)(2,1)} %get-tuple-element.64), channel_id=1, source_target_pairs={{0,25},{1,24},{8,17},{9,16},{16,9},{17,8},{24,1},{25,0},{2,27},{3,... | collective-permute-start | bytes 811016 | tf_op jit(solution)/shard_map/ppermute | solution.py:296
  25.6 1.1 %copy-start.1 = (bf16[1056,128]{1,0:T(8,128)(2,1)S(1)}, bf16[1056,128]{1,0:T(8,128)(2,1)}, u32[]{:S(2)}) copy-start(bf16[1056,128]{1,0:T(8,128)(2,1)} %get-tuple-element.53.refs_0_) | copy-start | bytes 811012
  26.7 5.4 %copy-start.2 = (bf16[4,272,128]{2,1,0:T(8,128)(2,1)S(1)}, bf16[4,272,128]{2,1,0:T(8,128)(2,1)}, u32[]{:S(2)}) copy-start(bf16[4,272,128]{2,1,0:T(8,128)(2,1)} %slice.13) | copy-start | bytes 835588
  32.1 21.3 %collective-permute-start.7 = (bf16[4,272,128]{2,1,0:T(8,128)(2,1)S(1)}, bf16[4,272,128]{2,1,0:T(8,128)(2,1)S(1)}, u32[]{:S(2)}, u32[]{:S(2)}) collective-permute-start(bf16[4,272,128]{2,1,0:T(8,128)(2,1)S(1)} %copy-done.2), channel_id=1, source_target_pairs={{0,4},{2,6},{4,0},{6,2},{1,5},{3,7},{5,1},{7,3},{8,12},{10,14},{12... | collective-permute-start | bytes 835592 | tf_op jit(solution)/shard_map/ppermute | solution.py:299
  48.9 27.7 %collective-permute-start.9 = (bf16[8,128,256]{2,1,0:T(8,128)(2,1)S(1)}, bf16[8,128,256]{2,1,0:T(8,128)(2,1)S(1)}, u32[]{:S(2)}, u32[]{:S(2)}) collective-permute-start(bf16[8,128,256]{2,1,0:T(8,128)(2,1)S(1)} %get-tuple-element.80), channel_id=1, source_target_pairs={{0,6},{2,0},{4,2},{6,4},{1,7},{3,1},{5,3},{7,5},{8,14},{10,8},{12,... | collective-permute-start | bytes 1572872 | tf_op jit(solution)/shard_map/ppermute | solution.py:299
  57.5 0.7 copy-start
  58.1 2.5 %collective-permute-start.11 = (bf16[512,128]{1,0:T(8,128)(2,1)S(1)}, bf16[512,128]{1,0:T(8,128)(2,1)S(1)}, u32[]{:S(2)}, u32[]{:S(2)}) collective-permute-start(bf16[512,128]{1,0:T(8,128)(2,1)S(1)} %get-tuple-element.82), channel_id=1, source_target_pairs={{0,8},{1,9},{8,0},{9,1},{16,24},{17,25},{24,16},{25,17},{2,10},{3,... | collective-permute-start | bytes 393224 | tf_op jit(solution)/shard_map/ppermute | solution.py:296
  59.2 6.4 %collective-permute-start.12 = (bf16[512,128]{1,0:T(8,128)(2,1)S(1)}, bf16[512,128]{1,0:T(8,128)(2,1)S(1)}, u32[]{:S(2)}, u32[]{:S(2)}) collective-permute-start(bf16[512,128]{1,0:T(8,128)(2,1)S(1)} %get-tuple-element.83), channel_id=1, source_target_pairs={{0,16},{1,17},{8,24},{9,25},{16,0},{17,1},{24,8},{25,9},{2,18},{3,... | collective-permute-start | bytes 393224 | tf_op jit(solution)/shard_map/ppermute | solution.py:296
  59.2 7.2 %collective-permute-start.13 = (bf16[512,128]{1,0:T(8,128)(2,1)S(1)}, bf16[512,128]{1,0:T(8,128)(2,1)S(1)}, u32[]{:S(2)}, u32[]{:S(2)}) collective-permute-start(bf16[512,128]{1,0:T(8,128)(2,1)S(1)} %get-tuple-element.84), channel_id=1, source_target_pairs={{0,24},{1,25},{8,16},{9,17},{16,8},{17,9},{24,0},{25,1},{2,26},{3,... | collective-permute-start | bytes 393224 | tf_op jit(solution)/shard_map/ppermute | solution.py:296
  60.6 6.2 %collective-permute-start.14 = (bf16[512,128]{1,0:T(8,128)(2,1)S(1)}, bf16[512,128]{1,0:T(8,128)(2,1)S(1)}, u32[]{:S(2)}, u32[]{:S(2)}) collective-permute-start(bf16[512,128]{1,0:T(8,128)(2,1)S(1)} %get-tuple-element.85), channel_id=1, source_target_pairs={{0,1},{1,0},{8,9},{9,8},{16,17},{17,16},{24,25},{25,24},{2,3},{3,2... | collective-permute-start | bytes 393224 | tf_op jit(solution)/shard_map/ppermute | solution.py:296
  60.6 17.0 %copy-start.3 = (bf16[512,128]{1,0:T(8,128)(2,1)}, bf16[512,128]{1,0:T(8,128)(2,1)S(1)}, u32[]{:S(2)}) copy-start(bf16[512,128]{1,0:T(8,128)(2,1)S(1)} %collective-permute-done.11.refs_1_) | copy-start | bytes 393220
  60.6 16.0 %collective-permute-start.10 = (bf16[4,128,256]{2,1,0:T(8,128)(2,1)S(1)}, bf16[4,128,256]{2,1,0:T(8,128)(2,1)S(1)}, u32[]{:S(2)}, u32[]{:S(2)}) collective-permute-start(bf16[4,128,256]{2,1,0:T(8,128)(2,1)S(1)} %get-tuple-element.81), channel_id=1, source_target_pairs={{0,4},{2,6},{4,0},{6,2},{1,5},{3,7},{5,1},{7,3},{8,12},{10,14},{12... | collective-permute-start | bytes 786440 | tf_op jit(solution)/shard_map/ppermute | solution.py:299
  65.6 11.9 %copy-start.4 = (bf16[512,128]{1,0:T(8,128)(2,1)}, bf16[512,128]{1,0:T(8,128)(2,1)S(1)}, u32[]{:S(2)}) copy-start(bf16[512,128]{1,0:T(8,128)(2,1)S(1)} %collective-permute-done.12.refs_2_) | copy-start | bytes 393220
  65.6 4.4 %collective-permute-start.15 = (bf16[512,128]{1,0:T(8,128)(2,1)S(1)}, bf16[512,128]{1,0:T(8,128)(2,1)S(1)}, u32[]{:S(2)}, u32[]{:S(2)}) collective-permute-start(bf16[512,128]{1,0:T(8,128)(2,1)S(1)} %get-tuple-element.86), channel_id=1, source_target_pairs={{0,9},{1,8},{8,1},{9,0},{16,25},{17,24},{24,17},{25,16},{2,11},{3,... | collective-permute-start | bytes 393224 | tf_op jit(solution)/shard_map/ppermute | solution.py:296
  66.5 11.1 %copy-start.5 = (bf16[512,128]{1,0:T(8,128)(2,1)}, bf16[512,128]{1,0:T(8,128)(2,1)S(1)}, u32[]{:S(2)}) copy-start(bf16[512,128]{1,0:T(8,128)(2,1)S(1)} %collective-permute-done.13.refs_3_) | copy-start | bytes 393220
  66.5 7.2 %collective-permute-start.16 = (bf16[512,128]{1,0:T(8,128)(2,1)S(1)}, bf16[512,128]{1,0:T(8,128)(2,1)S(1)}, u32[]{:S(2)}, u32[]{:S(2)}) collective-permute-start(bf16[512,128]{1,0:T(8,128)(2,1)S(1)} %get-tuple-element.87), channel_id=1, source_target_pairs={{0,17},{1,16},{8,25},{9,24},{16,1},{17,0},{24,9},{25,8},{2,19},{3,... | collective-permute-start | bytes 393224 | tf_op jit(solution)/shard_map/ppermute | solution.py:296
  66.8 10.8 %copy-start.6 = (bf16[512,128]{1,0:T(8,128)(2,1)}, bf16[512,128]{1,0:T(8,128)(2,1)S(1)}, u32[]{:S(2)}) copy-start(bf16[512,128]{1,0:T(8,128)(2,1)S(1)} %collective-permute-done.14.refs_4_) | copy-start | bytes 393220
  66.8 9.8 %collective-permute-start.17 = (bf16[512,128]{1,0:T(8,128)(2,1)S(1)}, bf16[512,128]{1,0:T(8,128)(2,1)S(1)}, u32[]{:S(2)}, u32[]{:S(2)}) collective-permute-start(bf16[512,128]{1,0:T(8,128)(2,1)S(1)} %get-tuple-element.88), channel_id=1, source_target_pairs={{0,25},{1,24},{8,17},{9,16},{16,9},{17,8},{24,1},{25,0},{2,27},{3,... | collective-permute-start | bytes 393224 | tf_op jit(solution)/shard_map/ppermute | solution.py:296
  70.0 7.6 %copy-start.7 = (bf16[512,128]{1,0:T(8,128)(2,1)}, bf16[512,128]{1,0:T(8,128)(2,1)S(1)}, u32[]{:S(2)}) copy-start(bf16[512,128]{1,0:T(8,128)(2,1)S(1)} %collective-permute-done.15.refs_5_) | copy-start | bytes 393220
  73.6 3.9 %copy-start.8 = (bf16[512,128]{1,0:T(8,128)(2,1)}, bf16[512,128]{1,0:T(8,128)(2,1)S(1)}, u32[]{:S(2)}) copy-start(bf16[512,128]{1,0:T(8,128)(2,1)S(1)} %collective-permute-done.16.refs_6_) | copy-start | bytes 393220
  76.6 1.0 %copy-start.9 = (bf16[512,128]{1,0:T(8,128)(2,1)}, bf16[512,128]{1,0:T(8,128)(2,1)S(1)}, u32[]{:S(2)}) copy-start(bf16[512,128]{1,0:T(8,128)(2,1)S(1)} %collective-permute-done.17.refs_7_) | copy-start | bytes 393220
  77.6 13.2 %all-to-all-start.1 = ((bf16[8,128,256]{2,1,0:T(8,128)(2,1)}), bf16[8,128,256]{2,1,0:T(8,128)(2,1)S(1)}, u32[]{:S(2)}, u32[]{:S(2)}) async-start(bf16[8,128,256]{2,1,0:T(8,128)(2,1)} %multiply_convert_fusion), calls=%async_computation.1 | async-start | bytes 1048576 | tf_op jit(solution)/shard_map/all_to_all | solution.py:302

commit v2 on v1

--- a/solution.py
+++ b/solution.py
@@ -268,14 +268,27 @@
         out_shape=jax.ShapeDtypeStruct((tokens, parts * width), BF16),
         in_specs=[SCALARS] + [WHOLE] * parts,
         out_specs=WHOLE,
+        compiler_params=pltpu.CompilerParams(vmem_limit_bytes=VMEM_LIMIT),
         name="unpack_queries",
     )(me, *grads)
 
 
 def unpack_kv(grads):
     parts, tokens = grads.shape[:2]
-    lines = lambda x: x.transpose(1, 0, 2).reshape(tokens, parts * HD)
-    return lines(grads[:, :, :HD]), lines(grads[:, :, HD:])
+
+    def kernel(in_ref, k_ref, v_ref):
+        for g in range(parts):
+            k_ref[:, g * HD : (g + 1) * HD] = in_ref[g, :, :HD]
+            v_ref[:, g * HD : (g + 1) * HD] = in_ref[g, :, HD:]
+
+    return pl.pallas_call(
+        kernel,
+        out_shape=[jax.ShapeDtypeStruct((tokens, parts * HD), BF16)] * 2,
+        in_specs=[WHOLE],
+        out_specs=[WHOLE] * 2,
+        compiler_params=pltpu.CompilerParams(vmem_limit_bytes=VMEM_LIMIT),
+        name="unpack_kv",
+    )(grads)
 
 
 def shards(sizes, query, keys, values, forward_out, out_grad, log_norm, tile_mask):

time: 93.7 us -> 91.6 us (0.978)
  waiting for transfers between devices: 26.9 us -> 29.8 us
  local copies, waits for them, and re-layouts: 3.92 us -> 1.04 us
  starting transfers between devices: 27.5 us -> 26 us
    ppermute x4, waiting for transfers between devices: 1.19 us -> 4.07 us  [along(): lax.ppermute(value, 'sup', [(i, (i + steps) % n_sup) for i in range(n_sup)])]
    unnamed x22 -> x4, local copies, waits for them, and re-layouts: 2.63 us -> 0.23 us
    pallas_call x1, Pallas kernels: 2.53 us -> 1.25 us  [unpack_queries(): pl.pallas_call(kernel, out_shape=jax.ShapeDtypeStruct((tokens, parts * wi...]
    ppermute x14, waiting for transfers between devices: 16.1 us -> 14.9 us  [swap(): return lax.ppermute(value, ('head', 'pair'), pairs)]
    all_to_all x2, waiting for transfers between devices: 9.58 us -> 10.8 us  [exchange(): lax.all_to_all(value, ('pair', 'head'), split_axis=0, concat_axis=0, tile...]
  transfers between devices with their start and end apart: 20 -> 20, of which waited for: 12 -> 11; matrix products, arithmetic and copies ran while one was open for 1% -> 1% of each run, Pallas kernels for 33% -> 32%
where the time goes in v2:
time: 91.6 us; the launch traced here: 91.1 us
  Pallas kernels  32.4 us (35%)
  waiting for transfers between devices  29.8 us (33%)
  starting transfers between devices  26 us (28%)
  other arithmetic  1.11 us (1%)
  local copies, waits for them, and re-layouts  1.04 us (1%)
    pallas_call x4, Pallas kernels, terms(): pl.pallas_call(kernel, out_shape=dq_shapes + acc_shapes, in_specs=[SCALAR...  21.5 us
    ppermute x14, waiting for transfers between devices, swap(): return lax.ppermute(value, ('head', 'pair'), pairs)  14.9 us
    all_to_all x2, waiting for transfers between devices, exchange(): lax.all_to_all(value, ('pair', 'head'), split_axis=0, concat_axis=0, tile...  10.8 us
    ppermute x14, starting transfers between devices, swap(): return lax.ppermute(value, ('head', 'pair'), pairs)  10.5 us
    all_to_all x2, starting transfers between devices, exchange(): lax.all_to_all(value, ('pair', 'head'), split_axis=0, concat_axis=0, tile...  8.66 us
    pallas_call x2, Pallas kernels, pack_queries(): pl.pallas_call(kernel, out_shape=[jax.ShapeDtypeStruct((rows, HD), BF16)]...  6.86 us
    ppermute x4, starting transfers between devices, along(): lax.ppermute(value, 'sup', [(i, (i + steps) % n_sup) for i in range(n_sup)])  6.83 us
    ppermute x4, waiting for transfers between devices, along(): lax.ppermute(value, 'sup', [(i, (i + steps) % n_sup) for i in range(n_sup)])  4.07 us
  transfers between devices with their start and end apart: 20, of which 11 were waited for; matrix products, arithmetic and copies ran while one was open for 1% of the time, Pallas kernels for 32%

profile of v2, /device:TPU:0, one launch (start us, length us, event | category | flops | bytes accessed | tf_op | source)
XLA Modules:
  0.0 91.1 jit_solution(9219225806700272774)
XLA Ops:
  0.6 1.9 %pack_kv.1 = bf16[8,272,128]{2,1,0:T(8,128)(2,1)} custom-call(bf16[128,1024]{1,0:T(8,128)(2,1)} %k_ref.1, bf16[128,1024]{1,0:T(8,128)(2,1)} %v_ref.1, s32[1,4,4,4]{3,2,1,0:T(4,128)} %m_ref.1), custom_call_target="tpu_custom_call" | custom-call | tf_op jit(solution)/shard_map/pack_kv/pallas_call | solution.py:43
  2.6 5.2 %all-to-all-start = ((bf16[8,272,128]{2,1,0:T(8,128)(2,1)}), bf16[8,272,128]{2,1,0:T(8,128)(2,1)S(1)}, u32[]{:S(2)}, u32[]{:S(2)}) async-start(bf16[8,272,128]{2,1,0:T(8,128)(2,1)} %pack_kv.1), calls=%async_computation | async-start | bytes 1114112 | tf_op jit(solution)/shard_map/all_to_all | solution.py:315
  7.7 4.5 %pack_queries.2 = (bf16[1056,128]{1,0:T(8,128)(2,1)}, bf16[1056,128]{1,0:T(8,128)(2,1)}, bf16[1056,128]{1,0:T(8,128)(2,1)}, bf16[1056,128]{1,0:T(8,128)(2,1)}, b...) custom-call(s32[1]{0:T(128)} %bitcast.me_ref, bf16[128,4096]{1,0:T(8,128)(2,1)} %q_ref.3, bf16[128,4096]{1,0:T(8,128)(2,1)} %g_ref.3, ...), custom_call_target="tpu_custom_call" | custom-call | tf_op jit(solution)/shard_map/pack_queries/pallas_call | solution.py:103
  12.8 1.7 %collective-permute-start.1 = (bf16[1056,128]{1,0:T(8,128)(2,1)}, bf16[1056,128]{1,0:T(8,128)(2,1)S(1)}, u32[]{:S(2)}, u32[]{:S(2)}) collective-permute-start(bf16[1056,128]{1,0:T(8,128)(2,1)} %get-tuple-element.59), channel_id=1, source_target_pairs={{0,16},{1,17},{8,24},{9,25},{16,0},{17,1},{24,8},{25,9},{2,18},{3,... | collective-permute-start | bytes 811016 | tf_op jit(solution)/shard_map/ppermute | solution.py:309
  14.5 1.5 %collective-permute-start.2 = (bf16[1056,128]{1,0:T(8,128)(2,1)}, bf16[1056,128]{1,0:T(8,128)(2,1)S(1)}, u32[]{:S(2)}, u32[]{:S(2)}) collective-permute-start(bf16[1056,128]{1,0:T(8,128)(2,1)} %get-tuple-element.60), channel_id=1, source_target_pairs={{0,1},{1,0},{8,9},{9,8},{16,17},{17,16},{24,25},{25,24},{2,3},{3,2... | collective-permute-start | bytes 811016 | tf_op jit(solution)/shard_map/ppermute | solution.py:309
  15.9 2.4 %all-to-all-done.refs_4_ = bf16[8,272,128]{2,1,0:T(8,128)(2,1)S(1)} async-done(((bf16[8,272,128]{2,1,0:T(8,128)(2,1)}), bf16[8,272,128]{2,1,0:T(8,128)(2,1)S(1)}, u32[]{:S(2)}, u32[]{:S(2)}) %all-to-all-start) | async-done | bytes 557088 | tf_op jit(solution)/shard_map/all_to_all | solution.py:315
  18.3 1.6 %collective-permute-start.8 = (bf16[8,272,128]{2,1,0:T(8,128)(2,1)S(1)}, bf16[8,272,128]{2,1,0:T(8,128)(2,1)S(1)}, u32[]{:S(2)}, u32[]{:S(2)}) collective-permute-start(bf16[8,272,128]{2,1,0:T(8,128)(2,1)S(1)} %all-to-all-done.refs_4_), channel_id=1, source_target_pairs={{0,2},{2,4},{4,6},{6,0},{1,3},{3,5},{5,7},{7,1},{8,10},{10,12},{12... | collective-permute-start | bytes 1671176 | tf_op jit(solution)/shard_map/ppermute | solution.py:312
  20.3 2.4 %pack_queries.3 = (bf16[1056,128]{1,0:T(8,128)(2,1)}, bf16[1056,128]{1,0:T(8,128)(2,1)}) custom-call(s32[1]{0:T(128)} %bitcast.me_ref, bf16[128,4096]{1,0:T(8,128)(2,1)} %q_ref.3, bf16[128,4096]{1,0:T(8,128)(2,1)} %g_ref.3, bf16[128,4096]{1,0:T(8,128)(2,1)} %f_ref.3, f32[8,4,128]{2,1,0:T(4,128)} %bitcast.5), custom_call_target="tpu_custom_call" | custom-call | tf_op jit(solution)/shard_map/pack_queries/pallas_call | solution.py:103
  22.7 1.3 %collective-permute-done.2.refs_3_.refs_4_ = bf16[1056,128]{1,0:T(8,128)(2,1)S(1)} collective-permute-done((bf16[1056,128]{1,0:T(8,128)(2,1)}, bf16[1056,128]{1,0:T(8,128)(2,1)S(1)}, u32[]{:S(2)}, u32[]{:S(2)}) %collective-permute-start.2) | collective-permute-done | bytes 270368 | tf_op jit(solution)/shard_map/ppermute | solution.py:309
  24.0 1.6 %collective-permute-start.5 = (bf16[1056,128]{1,0:T(8,128)(2,1)}, bf16[1056,128]{1,0:T(8,128)(2,1)S(1)}, u32[]{:S(2)}, u32[]{:S(2)}) collective-permute-start(bf16[1056,128]{1,0:T(8,128)(2,1)} %get-tuple-element.65), channel_id=1, source_target_pairs={{0,17},{1,16},{8,25},{9,24},{16,1},{17,0},{24,9},{25,8},{2,19},{3,... | collective-permute-start | bytes 811016 | tf_op jit(solution)/shard_map/ppermute | solution.py:309
  26.7 4.2 %terms.4 = (f32[128,512]{1,0:T(8,128)S(1)}, f32[128,512]{1,0:T(8,128)S(1)}, f32[128,512]{1,0:T(8,128)S(1)}, f32[128,512]{1,0:T(8,128)S(1)}, f32[8,128,256]{2,1,0:T(8,128)S(1)}) custom-call(s32[2]{0:T(128)S(1)} %pad_add_fusion.where_ref, s32[2,64]{1,0:T(2,128)S(1)} %reshape.30.mask_ref, bf16[1056,128]{1,0:T(8,128)(2,1)S(1)} %copy-done, ...), custom_call_target="tpu_custom_call" | custom-call | flops 1342177280 | bytes 1638400 | tf_op jit(solution)/shard_map/terms/pallas_call | solution.py:230
  30.9 1.3 %collective-permute-done.8.refs_4_.refs_5_ = bf16[8,272,128]{2,1,0:T(8,128)(2,1)S(1)} collective-permute-done((bf16[8,272,128]{2,1,0:T(8,128)(2,1)S(1)}, bf16[8,272,128]{2,1,0:T(8,128)(2,1)S(1)}, u32[]{:S(2)}, u32[]{:S(2)}) %collective-permute-start.8) | collective-permute-done | bytes 557088 | tf_op jit(solution)/shard_map/ppermute | solution.py:312
  32.1 0.7 collective-permute-start.7
  32.9 5.0 %terms.5 = (f32[128,512]{1,0:T(8,128)S(1)}, f32[128,512]{1,0:T(8,128)S(1)}, f32[128,512]{1,0:T(8,128)S(1)}, f32[128,512]{1,0:T(8,128)S(1)}, f32[8,128,256]{2,1,0:T(8,128)S(1)}) custom-call(s32[2]{0:T(128)S(1)} %pad_add_fusion.where_ref, s32[2,64]{1,0:T(2,128)S(1)} %reshape.30.mask_ref, bf16[1056,128]{1,0:T(8,128)(2,1)S(1)} %copy-done, ...), custom_call_target="tpu_custom_call" | custom-call | flops 1342177280 | bytes 2162688 | tf_op jit(solution)/shard_map/terms/pallas_call | solution.py:230
  37.8 1.8 %collective-permute-done.4.refs_1_.refs_5_ = bf16[1056,128]{1,0:T(8,128)(2,1)S(1)} collective-permute-done((bf16[1056,128]{1,0:T(8,128)(2,1)}, bf16[1056,128]{1,0:T(8,128)(2,1)S(1)}, u32[]{:S(2)}, u32[]{:S(2)}) %collective-permute-start.4) | collective-permute-done | bytes 270368 | tf_op jit(solution)/shard_map/ppermute | solution.py:309
  39.7 0.9 collective-permute-done.6.refs_3_.refs_7_
  40.5 9.1 %terms.6 = (f32[128,512]{1,0:T(8,128)S(1)}, f32[128,512]{1,0:T(8,128)S(1)}, f32[128,512]{1,0:T(8,128)S(1)}, f32[128,512]{1,0:T(8,128)S(1)}, f32[8,128,256]{2,1,0...) custom-call(s32[2]{0:T(128)S(1)} %pad_add_fusion.where_ref, s32[2,64]{1,0:T(2,128)S(1)} %reshape.30.mask_ref, ...), custom_call_target="tpu_custom_call" | custom-call | flops 2684354560 | bytes 3244032 | tf_op jit(solution)/shard_map/terms/pallas_call | solution.py:230
  49.7 2.9 %collective-permute-start.9 = (bf16[8,128,256]{2,1,0:T(8,128)(2,1)S(1)}, bf16[8,128,256]{2,1,0:T(8,128)(2,1)S(1)}, u32[]{:S(2)}, u32[]{:S(2)}) collective-permute-start(bf16[8,128,256]{2,1,0:T(8,128)(2,1)S(1)} %get-tuple-element.82), channel_id=1, source_target_pairs={{0,6},{2,0},{4,2},{6,4},{1,7},{3,1},{5,3},{7,5},{8,14},{10,8},{12,... | collective-permute-start | bytes 1572872 | tf_op jit(solution)/shard_map/ppermute | solution.py:312
  52.5 3.2 %terms.7 = (bf16[512,128]{1,0:T(8,128)(2,1)S(1)}, bf16[512,128]{1,0:T(8,128)(2,1)S(1)}, bf16[512,128]{1,0:T(8,128)(2,1)S(1)}, bf16[512,128]{1,0:T(8,128)(2,1)S(1...) custom-call(s32[2]{0:T(128)S(1)} %pad_add_fusion.where_ref, ...), custom_call_target="tpu_custom_call" | custom-call | flops 2684354560 | bytes 3489792 | tf_op jit(solution)/shard_map/terms/pallas_call | solution.py:230
  56.1 1.5 %collective-permute-start.13 = (bf16[512,128]{1,0:T(8,128)(2,1)S(1)}, bf16[512,128]{1,0:T(8,128)(2,1)S(1)}, u32[]{:S(2)}, u32[]{:S(2)}) collective-permute-start(bf16[512,128]{1,0:T(8,128)(2,1)S(1)} %get-tuple-element.86), channel_id=1, source_target_pairs={{0,24},{1,25},{8,16},{9,17},{16,8},{17,9},{24,0},{25,1},{2,26},{3,... | collective-permute-start | bytes 393224 | tf_op jit(solution)/shard_map/ppermute | solution.py:309
  57.8 1.7 %collective-permute-start.10 = (bf16[4,128,256]{2,1,0:T(8,128)(2,1)S(1)}, bf16[4,128,256]{2,1,0:T(8,128)(2,1)S(1)}, u32[]{:S(2)}, u32[]{:S(2)}) collective-permute-start(bf16[4,128,256]{2,1,0:T(8,128)(2,1)S(1)} %get-tuple-element.83), channel_id=1, source_target_pairs={{0,4},{2,6},{4,0},{6,2},{1,5},{3,7},{5,1},{7,3},{8,12},{10,14},{12... | collective-permute-start | bytes 786440 | tf_op jit(solution)/shard_map/ppermute | solution.py:312
  59.4 3.0 %collective-permute-done.12.refs_2_ = bf16[512,128]{1,0:T(8,128)(2,1)S(1)} collective-permute-done((bf16[512,128]{1,0:T(8,128)(2,1)S(1)}, bf16[512,128]{1,0:T(8,128)(2,1)S(1)}, u32[]{:S(2)}, u32[]{:S(2)}) %collective-permute-start.12) | collective-permute-done | bytes 131104 | tf_op jit(solution)/shard_map/ppermute | solution.py:309
  62.4 1.3 %collective-permute-done.13.refs_3_ = bf16[512,128]{1,0:T(8,128)(2,1)S(1)} collective-permute-done((bf16[512,128]{1,0:T(8,128)(2,1)S(1)}, bf16[512,128]{1,0:T(8,128)(2,1)S(1)}, u32[]{:S(2)}, u32[]{:S(2)}) %collective-permute-start.13) | collective-permute-done | bytes 131104 | tf_op jit(solution)/shard_map/ppermute | solution.py:309
  63.8 2.8 %collective-permute-start.17 = (bf16[512,128]{1,0:T(8,128)(2,1)S(1)}, bf16[512,128]{1,0:T(8,128)(2,1)S(1)}, u32[]{:S(2)}, u32[]{:S(2)}) collective-permute-start(bf16[512,128]{1,0:T(8,128)(2,1)S(1)} %get-tuple-element.90), channel_id=1, source_target_pairs={{0,25},{1,24},{8,17},{9,16},{16,9},{17,8},{24,1},{25,0},{2,27},{3,... | collective-permute-start | bytes 393224 | tf_op jit(solution)/shard_map/ppermute | solution.py:309
  66.6 5.0 %collective-permute-done.15.refs_5_ = bf16[512,128]{1,0:T(8,128)(2,1)S(1)} collective-permute-done((bf16[512,128]{1,0:T(8,128)(2,1)S(1)}, bf16[512,128]{1,0:T(8,128)(2,1)S(1)}, u32[]{:S(2)}, u32[]{:S(2)}) %collective-permute-start.15) | collective-permute-done | bytes 131104 | tf_op jit(solution)/shard_map/ppermute | solution.py:309
  71.6 1.5 %collective-permute-done.17.refs_7_ = bf16[512,128]{1,0:T(8,128)(2,1)S(1)} collective-permute-done((bf16[512,128]{1,0:T(8,128)(2,1)S(1)}, bf16[512,128]{1,0:T(8,128)(2,1)S(1)}, u32[]{:S(2)}, u32[]{:S(2)}) %collective-permute-start.17) | collective-permute-done | bytes 131104 | tf_op jit(solution)/shard_map/ppermute | solution.py:309
  73.1 2.8 %collective-permute-done.10 = bf16[4,128,256]{2,1,0:T(8,128)(2,1)S(1)} collective-permute-done((bf16[4,128,256]{2,1,0:T(8,128)(2,1)S(1)}, bf16[4,128,256]{2,1,0:T(8,128)(2,1)S(1)}, u32[]{:S(2)}, u32[]{:S(2)}) %collective-permute-start.10) | collective-permute-done | bytes 262176 | tf_op jit(solution)/shard_map/ppermute | solution.py:312
  75.9 1.0 %multiply_convert_fusion = bf16[8,128,256]{2,1,0:T(8,128)(2,1)} fusion(f32[8,128,256]{2,1,0:T(8,128)S(1)} %get-tuple-element.98, bf16[8,128,256]{2,1,0:T(8,128)(2,1)S(1)} %collective-permute-done.9, f32[256]{0:T(256)S(1)} %compare_select_fusion, bf16[4,128,256]{2,1,0:T(8,128)(2,1)S(1)} %collective-permute-done.10), kind=kLoop, calls=%fused_computation | loop fusion | flops 1572864 | bytes 2360320 | tf_op jit(solution)/shard_map/convert_element_type | solution.py:251
  77.0 3.5 %all-to-all-start.1 = ((bf16[8,128,256]{2,1,0:T(8,128)(2,1)}), bf16[8,128,256]{2,1,0:T(8,128)(2,1)S(1)}, u32[]{:S(2)}, u32[]{:S(2)}) async-start(bf16[8,128,256]{2,1,0:T(8,128)(2,1)} %multiply_convert_fusion), calls=%async_computation.1 | async-start | bytes 1048576 | tf_op jit(solution)/shard_map/all_to_all | solution.py:315
  80.5 1.2 %unpack_queries.1 = bf16[128,4096]{1,0:T(8,128)(2,1)} custom-call(s32[1]{0:T(128)} %bitcast.me_ref, bf16[512,128]{1,0:T(8,128)(2,1)S(1)} %get-tuple-element.81.refs_0_, bf16[512,128]{1,0:T(8,128)(2,1)S(1)} %collective-permute-done.11.refs_1_, bf16[512,128]{1,0:T(8,128)(2,1)S(1)} %collective-permute-done.12.refs_2_, ...), custom_call_target="tpu_custom_call" | custom-call | tf_op jit(solution)/shard_map/unpack_queries/pallas_call | solution.py:266
  81.7 8.4 %all-to-all-done.1.in_ref = bf16[8,128,256]{2,1,0:T(8,128)(2,1)S(1)} async-done(((bf16[8,128,256]{2,1,0:T(8,128)(2,1)}), bf16[8,128,256]{2,1,0:T(8,128)(2,1)S(1)}, u32[]{:S(2)}, u32[]{:S(2)}) %all-to-all-start.1) | async-done | bytes 524320 | tf_op jit(solution)/shard_map/all_to_all | solution.py:315
  90.1 0.9 %unpack_kv.1 = (bf16[128,1024]{1,0:T(8,128)(2,1)}, bf16[128,1024]{1,0:T(8,128)(2,1)}) custom-call(bf16[8,128,256]{2,1,0:T(8,128)(2,1)S(1)} %all-to-all-done.1.in_ref), custom_call_target="tpu_custom_call" | custom-call | tf_op jit(solution)/shard_map/unpack_kv/pallas_call | solution.py:284
  (27 shorter events, 2.6 us)
Async XLA Ops:
  2.6 15.7 %all-to-all-start = ((bf16[8,272,128]{2,1,0:T(8,128)(2,1)}), bf16[8,272,128]{2,1,0:T(8,128)(2,1)S(1)}, u32[]{:S(2)}, u32[]{:S(2)}) async-start(bf16[8,272,128]{2,1,0:T(8,128)(2,1)} %pack_kv.1), calls=%async_computation | async-start | bytes 1114112 | tf_op jit(solution)/shard_map/all_to_all | solution.py:315
  12.2 3.7 %collective-permute-start = (bf16[1056,128]{1,0:T(8,128)(2,1)}, bf16[1056,128]{1,0:T(8,128)(2,1)S(1)}, u32[]{:S(2)}, u32[]{:S(2)}) collective-permute-start(bf16[1056,128]{1,0:T(8,128)(2,1)} %get-tuple-element.53), channel_id=1, source_target_pairs={{0,8},{1,9},{8,0},{9,1},{16,24},{17,25},{24,16},{25,17},{2,10},{3,... | collective-permute-start | bytes 811016 | tf_op jit(solution)/shard_map/ppermute | solution.py:309
  12.8 9.9 %collective-permute-start.1 = (bf16[1056,128]{1,0:T(8,128)(2,1)}, bf16[1056,128]{1,0:T(8,128)(2,1)S(1)}, u32[]{:S(2)}, u32[]{:S(2)}) collective-permute-start(bf16[1056,128]{1,0:T(8,128)(2,1)} %get-tuple-element.59), channel_id=1, source_target_pairs={{0,16},{1,17},{8,24},{9,25},{16,0},{17,1},{24,8},{25,9},{2,18},{3,... | collective-permute-start | bytes 811016 | tf_op jit(solution)/shard_map/ppermute | solution.py:309
  14.5 9.6 %collective-permute-start.2 = (bf16[1056,128]{1,0:T(8,128)(2,1)}, bf16[1056,128]{1,0:T(8,128)(2,1)S(1)}, u32[]{:S(2)}, u32[]{:S(2)}) collective-permute-start(bf16[1056,128]{1,0:T(8,128)(2,1)} %get-tuple-element.60), channel_id=1, source_target_pairs={{0,1},{1,0},{8,9},{9,8},{16,17},{17,16},{24,25},{25,24},{2,3},{3,2... | collective-permute-start | bytes 811016 | tf_op jit(solution)/shard_map/ppermute | solution.py:309
  18.3 13.8 %collective-permute-start.8 = (bf16[8,272,128]{2,1,0:T(8,128)(2,1)S(1)}, bf16[8,272,128]{2,1,0:T(8,128)(2,1)S(1)}, u32[]{:S(2)}, u32[]{:S(2)}) collective-permute-start(bf16[8,272,128]{2,1,0:T(8,128)(2,1)S(1)} %all-to-all-done.refs_4_), channel_id=1, source_target_pairs={{0,2},{2,4},{4,6},{6,0},{1,3},{3,5},{5,7},{7,1},{8,10},{10,12},{12... | collective-permute-start | bytes 1671176 | tf_op jit(solution)/shard_map/ppermute | solution.py:312
  19.9 17.9 %collective-permute-start.3 = (bf16[1056,128]{1,0:T(8,128)(2,1)}, bf16[1056,128]{1,0:T(8,128)(2,1)S(1)}, u32[]{:S(2)}, u32[]{:S(2)}) collective-permute-start(bf16[1056,128]{1,0:T(8,128)(2,1)} %get-tuple-element.62), channel_id=1, source_target_pairs={{0,24},{1,25},{8,16},{9,17},{16,8},{17,9},{24,0},{25,1},{2,26},{3,... | collective-permute-start | bytes 811016 | tf_op jit(solution)/shard_map/ppermute | solution.py:309
  19.9 19.8 %collective-permute-start.4 = (bf16[1056,128]{1,0:T(8,128)(2,1)}, bf16[1056,128]{1,0:T(8,128)(2,1)S(1)}, u32[]{:S(2)}, u32[]{:S(2)}) collective-permute-start(bf16[1056,128]{1,0:T(8,128)(2,1)} %get-tuple-element.64), channel_id=1, source_target_pairs={{0,9},{1,8},{8,1},{9,0},{16,25},{17,24},{24,17},{25,16},{2,11},{3,... | collective-permute-start | bytes 811016 | tf_op jit(solution)/shard_map/ppermute | solution.py:309
  24.0 15.6 %collective-permute-start.5 = (bf16[1056,128]{1,0:T(8,128)(2,1)}, bf16[1056,128]{1,0:T(8,128)(2,1)S(1)}, u32[]{:S(2)}, u32[]{:S(2)}) collective-permute-start(bf16[1056,128]{1,0:T(8,128)(2,1)} %get-tuple-element.65), channel_id=1, source_target_pairs={{0,17},{1,16},{8,25},{9,24},{16,1},{17,0},{24,9},{25,8},{2,19},{3,... | collective-permute-start | bytes 811016 | tf_op jit(solution)/shard_map/ppermute | solution.py:309
  25.6 14.9 %collective-permute-start.6 = (bf16[1056,128]{1,0:T(8,128)(2,1)}, bf16[1056,128]{1,0:T(8,128)(2,1)S(1)}, u32[]{:S(2)}, u32[]{:S(2)}) collective-permute-start(bf16[1056,128]{1,0:T(8,128)(2,1)} %get-tuple-element.66), channel_id=1, source_target_pairs={{0,25},{1,24},{8,17},{9,16},{16,9},{17,8},{24,1},{25,0},{2,27},{3,... | collective-permute-start | bytes 811016 | tf_op jit(solution)/shard_map/ppermute | solution.py:309
  25.6 1.0 %copy-start = (bf16[1056,128]{1,0:T(8,128)(2,1)S(1)}, bf16[1056,128]{1,0:T(8,128)(2,1)}, u32[]{:S(2)}) copy-start(bf16[1056,128]{1,0:T(8,128)(2,1)} %get-tuple-element.55.refs_0_) | copy-start | bytes 811012
  26.7 5.4 %copy-start.1 = (bf16[4,272,128]{2,1,0:T(8,128)(2,1)S(1)}, bf16[4,272,128]{2,1,0:T(8,128)(2,1)}, u32[]{:S(2)}) copy-start(bf16[4,272,128]{2,1,0:T(8,128)(2,1)} %slice.7) | copy-start | bytes 835588
  32.1 20.4 %collective-permute-start.7 = (bf16[4,272,128]{2,1,0:T(8,128)(2,1)S(1)}, bf16[4,272,128]{2,1,0:T(8,128)(2,1)S(1)}, u32[]{:S(2)}, u32[]{:S(2)}) collective-permute-start(bf16[4,272,128]{2,1,0:T(8,128)(2,1)S(1)} %copy-done.1), channel_id=1, source_target_pairs={{0,4},{2,6},{4,0},{6,2},{1,5},{3,7},{5,1},{7,3},{8,12},{10,14},{12... | collective-permute-start | bytes 835592 | tf_op jit(solution)/shard_map/ppermute | solution.py:312
  49.7 26.3 %collective-permute-start.9 = (bf16[8,128,256]{2,1,0:T(8,128)(2,1)S(1)}, bf16[8,128,256]{2,1,0:T(8,128)(2,1)S(1)}, u32[]{:S(2)}, u32[]{:S(2)}) collective-permute-start(bf16[8,128,256]{2,1,0:T(8,128)(2,1)S(1)} %get-tuple-element.82), channel_id=1, source_target_pairs={{0,6},{2,0},{4,2},{6,4},{1,7},{3,1},{5,3},{7,5},{8,14},{10,8},{12,... | collective-permute-start | bytes 1572872 | tf_op jit(solution)/shard_map/ppermute | solution.py:312
  55.7 2.0 %collective-permute-start.11 = (bf16[512,128]{1,0:T(8,128)(2,1)S(1)}, bf16[512,128]{1,0:T(8,128)(2,1)S(1)}, u32[]{:S(2)}, u32[]{:S(2)}) collective-permute-start(bf16[512,128]{1,0:T(8,128)(2,1)S(1)} %get-tuple-element.84), channel_id=1, source_target_pairs={{0,8},{1,9},{8,0},{9,1},{16,24},{17,25},{24,16},{25,17},{2,10},{3,... | collective-permute-start | bytes 393224 | tf_op jit(solution)/shard_map/ppermute | solution.py:309
  56.1 6.3 %collective-permute-start.12 = (bf16[512,128]{1,0:T(8,128)(2,1)S(1)}, bf16[512,128]{1,0:T(8,128)(2,1)S(1)}, u32[]{:S(2)}, u32[]{:S(2)}) collective-permute-start(bf16[512,128]{1,0:T(8,128)(2,1)S(1)} %get-tuple-element.85), channel_id=1, source_target_pairs={{0,16},{1,17},{8,24},{9,25},{16,0},{17,1},{24,8},{25,9},{2,18},{3,... | collective-permute-start | bytes 393224 | tf_op jit(solution)/shard_map/ppermute | solution.py:309
  56.1 7.7 %collective-permute-start.13 = (bf16[512,128]{1,0:T(8,128)(2,1)S(1)}, bf16[512,128]{1,0:T(8,128)(2,1)S(1)}, u32[]{:S(2)}, u32[]{:S(2)}) collective-permute-start(bf16[512,128]{1,0:T(8,128)(2,1)S(1)} %get-tuple-element.86), channel_id=1, source_target_pairs={{0,24},{1,25},{8,16},{9,17},{16,8},{17,9},{24,0},{25,1},{2,26},{3,... | collective-permute-start | bytes 393224 | tf_op jit(solution)/shard_map/ppermute | solution.py:309
  57.6 6.1 %collective-permute-start.14 = (bf16[512,128]{1,0:T(8,128)(2,1)S(1)}, bf16[512,128]{1,0:T(8,128)(2,1)S(1)}, u32[]{:S(2)}, u32[]{:S(2)}) collective-permute-start(bf16[512,128]{1,0:T(8,128)(2,1)S(1)} %get-tuple-element.87), channel_id=1, source_target_pairs={{0,1},{1,0},{8,9},{9,8},{16,17},{17,16},{24,25},{25,24},{2,3},{3,2... | collective-permute-start | bytes 393224 | tf_op jit(solution)/shard_map/ppermute | solution.py:309
  57.8 18.2 %collective-permute-start.10 = (bf16[4,128,256]{2,1,0:T(8,128)(2,1)S(1)}, bf16[4,128,256]{2,1,0:T(8,128)(2,1)S(1)}, u32[]{:S(2)}, u32[]{:S(2)}) collective-permute-start(bf16[4,128,256]{2,1,0:T(8,128)(2,1)S(1)} %get-tuple-element.83), channel_id=1, source_target_pairs={{0,4},{2,6},{4,0},{6,2},{1,5},{3,7},{5,1},{7,3},{8,12},{10,14},{12... | collective-permute-start | bytes 786440 | tf_op jit(solution)/shard_map/ppermute | solution.py:312
  62.4 9.2 %collective-permute-start.15 = (bf16[512,128]{1,0:T(8,128)(2,1)S(1)}, bf16[512,128]{1,0:T(8,128)(2,1)S(1)}, u32[]{:S(2)}, u32[]{:S(2)}) collective-permute-start(bf16[512,128]{1,0:T(8,128)(2,1)S(1)} %get-tuple-element.88), channel_id=1, source_target_pairs={{0,9},{1,8},{8,1},{9,0},{16,25},{17,24},{24,17},{25,16},{2,11},{3,... | collective-permute-start | bytes 393224 | tf_op jit(solution)/shard_map/ppermute | solution.py:309
  63.8 7.9 %collective-permute-start.16 = (bf16[512,128]{1,0:T(8,128)(2,1)S(1)}, bf16[512,128]{1,0:T(8,128)(2,1)S(1)}, u32[]{:S(2)}, u32[]{:S(2)}) collective-permute-start(bf16[512,128]{1,0:T(8,128)(2,1)S(1)} %get-tuple-element.89), channel_id=1, source_target_pairs={{0,17},{1,16},{8,25},{9,24},{16,1},{17,0},{24,9},{25,8},{2,19},{3,... | collective-permute-start | bytes 393224 | tf_op jit(solution)/shard_map/ppermute | solution.py:309
  63.8 9.3 %collective-permute-start.17 = (bf16[512,128]{1,0:T(8,128)(2,1)S(1)}, bf16[512,128]{1,0:T(8,128)(2,1)S(1)}, u32[]{:S(2)}, u32[]{:S(2)}) collective-permute-start(bf16[512,128]{1,0:T(8,128)(2,1)S(1)} %get-tuple-element.90), channel_id=1, source_target_pairs={{0,25},{1,24},{8,17},{9,16},{16,9},{17,8},{24,1},{25,0},{2,27},{3,... | collective-permute-start | bytes 393224 | tf_op jit(solution)/shard_map/ppermute | solution.py:309
  77.0 13.2 %all-to-all-start.1 = ((bf16[8,128,256]{2,1,0:T(8,128)(2,1)}), bf16[8,128,256]{2,1,0:T(8,128)(2,1)S(1)}, u32[]{:S(2)}, u32[]{:S(2)}) async-start(bf16[8,128,256]{2,1,0:T(8,128)(2,1)} %multiply_convert_fusion), calls=%async_computation.1 | async-start | bytes 1048576 | tf_op jit(solution)/shard_map/all_to_all | solution.py:315

commit v3 on v2

--- a/solution.py
+++ b/solution.py
@@ -14,7 +14,7 @@
 LOG2E = 1.4426950408889634
 F32 = jnp.float32
 BF16 = jnp.bfloat16
-EXTRA = 32
+EXTRA = 16
 VMEM_LIMIT = 16 * 1024 * 1024
 VMEM_ALL = 60 * 1024 * 1024
 
@@ -50,12 +50,9 @@
     )(keys, values, tile_mask)
 
 
-def split3(x):
+def split2(x):
     a = x.astype(BF16)
-    r = x - a.astype(F32)
-    b = r.astype(BF16)
-    c = (r - b.astype(F32)).astype(BF16)
-    return a, b, c
+    return a, (x - a.astype(F32)).astype(BF16)
 
 
 def pack_queries(me, query, out_grad, forward_out, log_norm, parts, offsets):
@@ -85,7 +82,6 @@
         line = lax.broadcasted_iota(jnp.int32, (16, width), 0)
         lane = lax.broadcasted_iota(jnp.int32, (16, width), 1)
         pick = jnp.where(lane // HD == line, 1.0, 0.0).astype(BF16)
-        pad = jnp.zeros((EXTRA - 6 * heads, tokens), BF16)
         n_load.wait()
         for s, (d, out) in enumerate(zip(offsets, outs)):
             for copy in loads[s]:
@@ -98,7 +94,7 @@
             for h in range(heads):
                 out[h * tokens : (h + 1) * tokens, :] = q_buf[s, :, h * HD : (h + 1) * HD]
                 out[(heads + h) * tokens : (heads + h + 1) * tokens, :] = g_buf[s, :, h * HD : (h + 1) * HD]
-            out[2 * heads * tokens :, :] = jnp.concatenate(split3(norm) + split3(delta) + (pad,), axis=0)
+            out[2 * heads * tokens :, :] = jnp.concatenate(split2(norm) + split2(delta), axis=0)
 
     return pl.pallas_call(
         kernel,
@@ -164,8 +160,8 @@
             q_buf[slot] = q_ref[: 2 * rows, :]
             extra = q_ref[2 * rows :, :].astype(F32)
             piece = lambda k: extra[k * heads : (k + 1) * heads]
-            line_buf[slot, 0:1, :] = side_by_side(piece(0) + piece(1) + piece(2)) * LOG2E
-            line_buf[slot, 1:2, :] = side_by_side(piece(3) + piece(4) + piece(5))
+            line_buf[slot, 0:1, :] = side_by_side(piece(0) + piece(1)) * LOG2E
+            line_buf[slot, 1:2, :] = side_by_side(piece(2) + piece(3))
             dq_acc[slot] = dq_old[d][...] if d in dq_old else jnp.zeros((HD, rows), F32)
             other = jnp.bitwise_xor(pair, d // tiles)
             row = jnp.bitwise_xor(head, d % tiles)

time: 91.6 us -> 91.5 us (level)
    ppermute x14, starting transfers between devices: 10.5 us -> 12 us  [swap(): return lax.ppermute(value, ('head', 'pair'), pairs)]
    ppermute x4, starting transfers between devices: 6.83 us -> 5.82 us  [along(): lax.ppermute(value, 'sup', [(i, (i + steps) % n_sup) for i in range(n_sup)])]
  transfers between devices with their start and end apart: 20 -> 20, of which waited for: 11 -> 10; matrix products, arithmetic and copies ran while one was open for 1% -> 1% of each run, Pallas kernels for 32% -> 32%
where the time goes in v3:
time: 91.5 us; the launch traced here: 91.8 us
  Pallas kernels  32.5 us (36%)
  waiting for transfers between devices  30 us (33%)
  starting transfers between devices  26.4 us (29%)
  other arithmetic  1.11 us (1%)
  local copies, waits for them, and re-layouts  1.04 us (1%)
    pallas_call x4, Pallas kernels, terms(): pl.pallas_call(kernel, out_shape=dq_shapes + acc_shapes, in_specs=[SCALAR...  21.6 us
    ppermute x14, waiting for transfers between devices, swap(): return lax.ppermute(value, ('head', 'pair'), pairs)  14.6 us
    ppermute x14, starting transfers between devices, swap(): return lax.ppermute(value, ('head', 'pair'), pairs)  12 us
    all_to_all x2, waiting for transfers between devices, exchange(): lax.all_to_all(value, ('pair', 'head'), split_axis=0, concat_axis=0, tile...  10.8 us
    all_to_all x2, starting transfers between devices, exchange(): lax.all_to_all(value, ('pair', 'head'), split_axis=0, concat_axis=0, tile...  8.66 us
    pallas_call x2, Pallas kernels, pack_queries(): pl.pallas_call(kernel, out_shape=[jax.ShapeDtypeStruct((rows, HD), BF16)]...  6.82 us
    ppermute x4, starting transfers between devices, along(): lax.ppermute(value, 'sup', [(i, (i + steps) % n_sup) for i in range(n_sup)])  5.82 us
    ppermute x4, waiting for transfers between devices, along(): lax.ppermute(value, 'sup', [(i, (i + steps) % n_sup) for i in range(n_sup)])  4.54 us
  transfers between devices with their start and end apart: 20, of which 10 were waited for; matrix products, arithmetic and copies ran while one was open for 1% of the time, Pallas kernels for 32%

profile of v3, /device:TPU:0, one launch (start us, length us, event | category | flops | bytes accessed | tf_op | source)
XLA Modules:
  0.0 91.8 jit_solution(14804021186281423299)
XLA Ops:
  0.6 1.9 %pack_kv.1 = bf16[8,272,128]{2,1,0:T(8,128)(2,1)} custom-call(bf16[128,1024]{1,0:T(8,128)(2,1)} %k_ref.1, bf16[128,1024]{1,0:T(8,128)(2,1)} %v_ref.1, s32[1,4,4,4]{3,2,1,0:T(4,128)} %m_ref.1), custom_call_target="tpu_custom_call" | custom-call | tf_op jit(solution)/shard_map/pack_kv/pallas_call | solution.py:43
  2.6 5.2 %all-to-all-start = ((bf16[8,272,128]{2,1,0:T(8,128)(2,1)}), bf16[8,272,128]{2,1,0:T(8,128)(2,1)S(1)}, u32[]{:S(2)}, u32[]{:S(2)}) async-start(bf16[8,272,128]{2,1,0:T(8,128)(2,1)} %pack_kv.1), calls=%async_computation | async-start | bytes 1114112 | tf_op jit(solution)/shard_map/all_to_all | solution.py:311
  7.7 4.4 %pack_queries.2 = (bf16[1040,128]{1,0:T(8,128)(2,1)}, bf16[1040,128]{1,0:T(8,128)(2,1)}, bf16[1040,128]{1,0:T(8,128)(2,1)}, bf16[1040,128]{1,0:T(8,128)(2,1)}, b...) custom-call(s32[1]{0:T(128)} %bitcast.me_ref, bf16[128,4096]{1,0:T(8,128)(2,1)} %q_ref.3, bf16[128,4096]{1,0:T(8,128)(2,1)} %g_ref.3, ...), custom_call_target="tpu_custom_call" | custom-call | tf_op jit(solution)/shard_map/pack_queries/pallas_call | solution.py:99
  12.8 1.7 %collective-permute-start.1 = (bf16[1040,128]{1,0:T(8,128)(2,1)}, bf16[1040,128]{1,0:T(8,128)(2,1)S(1)}, u32[]{:S(2)}, u32[]{:S(2)}) collective-permute-start(bf16[1040,128]{1,0:T(8,128)(2,1)} %get-tuple-element.59), channel_id=1, source_target_pairs={{0,16},{1,17},{8,24},{9,25},{16,0},{17,1},{24,8},{25,9},{2,18},{3,... | collective-permute-start | bytes 798728 | tf_op jit(solution)/shard_map/ppermute | solution.py:305
  14.4 1.5 %collective-permute-start.2 = (bf16[1040,128]{1,0:T(8,128)(2,1)}, bf16[1040,128]{1,0:T(8,128)(2,1)S(1)}, u32[]{:S(2)}, u32[]{:S(2)}) collective-permute-start(bf16[1040,128]{1,0:T(8,128)(2,1)} %get-tuple-element.60), channel_id=1, source_target_pairs={{0,1},{1,0},{8,9},{9,8},{16,17},{17,16},{24,25},{25,24},{2,3},{3,2... | collective-permute-start | bytes 798728 | tf_op jit(solution)/shard_map/ppermute | solution.py:305
  15.9 2.4 %all-to-all-done.refs_4_ = bf16[8,272,128]{2,1,0:T(8,128)(2,1)S(1)} async-done(((bf16[8,272,128]{2,1,0:T(8,128)(2,1)}), bf16[8,272,128]{2,1,0:T(8,128)(2,1)S(1)}, u32[]{:S(2)}, u32[]{:S(2)}) %all-to-all-start) | async-done | bytes 557088 | tf_op jit(solution)/shard_map/all_to_all | solution.py:311
  18.3 1.6 %collective-permute-start.8 = (bf16[8,272,128]{2,1,0:T(8,128)(2,1)S(1)}, bf16[8,272,128]{2,1,0:T(8,128)(2,1)S(1)}, u32[]{:S(2)}, u32[]{:S(2)}) collective-permute-start(bf16[8,272,128]{2,1,0:T(8,128)(2,1)S(1)} %all-to-all-done.refs_4_), channel_id=1, source_target_pairs={{0,2},{2,4},{4,6},{6,0},{1,3},{3,5},{5,7},{7,1},{8,10},{10,12},{12... | collective-permute-start | bytes 1671176 | tf_op jit(solution)/shard_map/ppermute | solution.py:308
  20.3 2.4 %pack_queries.3 = (bf16[1040,128]{1,0:T(8,128)(2,1)}, bf16[1040,128]{1,0:T(8,128)(2,1)}) custom-call(s32[1]{0:T(128)} %bitcast.me_ref, bf16[128,4096]{1,0:T(8,128)(2,1)} %q_ref.3, bf16[128,4096]{1,0:T(8,128)(2,1)} %g_ref.3, bf16[128,4096]{1,0:T(8,128)(2,1)} %f_ref.3, f32[8,4,128]{2,1,0:T(4,128)} %bitcast.5), custom_call_target="tpu_custom_call" | custom-call | tf_op jit(solution)/shard_map/pack_queries/pallas_call | solution.py:99
  22.7 1.2 %collective-permute-done.2.refs_3_.refs_4_ = bf16[1040,128]{1,0:T(8,128)(2,1)S(1)} collective-permute-done((bf16[1040,128]{1,0:T(8,128)(2,1)}, bf16[1040,128]{1,0:T(8,128)(2,1)S(1)}, u32[]{:S(2)}, u32[]{:S(2)}) %collective-permute-start.2) | collective-permute-done | bytes 266272 | tf_op jit(solution)/shard_map/ppermute | solution.py:305
  23.9 1.6 %collective-permute-start.5 = (bf16[1040,128]{1,0:T(8,128)(2,1)}, bf16[1040,128]{1,0:T(8,128)(2,1)S(1)}, u32[]{:S(2)}, u32[]{:S(2)}) collective-permute-start(bf16[1040,128]{1,0:T(8,128)(2,1)} %get-tuple-element.65), channel_id=1, source_target_pairs={{0,17},{1,16},{8,25},{9,24},{16,1},{17,0},{24,9},{25,8},{2,19},{3,... | collective-permute-start | bytes 798728 | tf_op jit(solution)/shard_map/ppermute | solution.py:305
  26.7 3.4 %terms.4 = (f32[128,512]{1,0:T(8,128)S(1)}, f32[128,512]{1,0:T(8,128)S(1)}, f32[128,512]{1,0:T(8,128)S(1)}, f32[128,512]{1,0:T(8,128)S(1)}, f32[8,128,256]{2,1,0:T(8,128)S(1)}) custom-call(s32[2]{0:T(128)S(1)} %pad_add_fusion.where_ref, s32[2,64]{1,0:T(2,128)S(1)} %reshape.30.mask_ref, bf16[1040,128]{1,0:T(8,128)(2,1)S(1)} %copy-done, ...), custom_call_target="tpu_custom_call" | custom-call | flops 1342177280 | bytes 1622016 | tf_op jit(solution)/shard_map/terms/pallas_call | solution.py:226
  30.0 2.1 %collective-permute-done.8.refs_4_.refs_5_ = bf16[8,272,128]{2,1,0:T(8,128)(2,1)S(1)} collective-permute-done((bf16[8,272,128]{2,1,0:T(8,128)(2,1)S(1)}, bf16[8,272,128]{2,1,0:T(8,128)(2,1)S(1)}, u32[]{:S(2)}, u32[]{:S(2)}) %collective-permute-start.8) | collective-permute-done | bytes 557088 | tf_op jit(solution)/shard_map/ppermute | solution.py:308
  32.1 1.4 %collective-permute-start.7 = (bf16[4,272,128]{2,1,0:T(8,128)(2,1)S(1)}, bf16[4,272,128]{2,1,0:T(8,128)(2,1)S(1)}, u32[]{:S(2)}, u32[]{:S(2)}) collective-permute-start(bf16[4,272,128]{2,1,0:T(8,128)(2,1)S(1)} %copy-done.1), channel_id=1, source_target_pairs={{0,4},{2,6},{4,0},{6,2},{1,5},{3,7},{5,1},{7,3},{8,12},{10,14},{12... | collective-permute-start | bytes 835592 | tf_op jit(solution)/shard_map/ppermute | solution.py:308
  33.5 5.0 %terms.5 = (f32[128,512]{1,0:T(8,128)S(1)}, f32[128,512]{1,0:T(8,128)S(1)}, f32[128,512]{1,0:T(8,128)S(1)}, f32[128,512]{1,0:T(8,128)S(1)}, f32[8,128,256]{2,1,0:T(8,128)S(1)}) custom-call(s32[2]{0:T(128)S(1)} %pad_add_fusion.where_ref, s32[2,64]{1,0:T(2,128)S(1)} %reshape.30.mask_ref, bf16[1040,128]{1,0:T(8,128)(2,1)S(1)} %copy-done, ...), custom_call_target="tpu_custom_call" | custom-call | flops 1342177280 | bytes 2146304 | tf_op jit(solution)/shard_map/terms/pallas_call | solution.py:226
  38.5 0.8 collective-permute-done.4.refs_1_.refs_5_
  39.3 1.0 %collective-permute-done.6.refs_3_.refs_7_ = bf16[1040,128]{1,0:T(8,128)(2,1)S(1)} collective-permute-done((bf16[1040,128]{1,0:T(8,128)(2,1)}, bf16[1040,128]{1,0:T(8,128)(2,1)S(1)}, u32[]{:S(2)}, u32[]{:S(2)}) %collective-permute-start.6) | collective-permute-done | bytes 266272 | tf_op jit(solution)/shard_map/ppermute | solution.py:305
  40.3 9.1 %terms.6 = (f32[128,512]{1,0:T(8,128)S(1)}, f32[128,512]{1,0:T(8,128)S(1)}, f32[128,512]{1,0:T(8,128)S(1)}, f32[128,512]{1,0:T(8,128)S(1)}, f32[8,128,256]{2,1,0...) custom-call(s32[2]{0:T(128)S(1)} %pad_add_fusion.where_ref, s32[2,64]{1,0:T(2,128)S(1)} %reshape.30.mask_ref, ...), custom_call_target="tpu_custom_call" | custom-call | flops 2684354560 | bytes 3227648 | tf_op jit(solution)/shard_map/terms/pallas_call | solution.py:226
  49.4 2.8 %collective-permute-start.9 = (bf16[8,128,256]{2,1,0:T(8,128)(2,1)S(1)}, bf16[8,128,256]{2,1,0:T(8,128)(2,1)S(1)}, u32[]{:S(2)}, u32[]{:S(2)}) collective-permute-start(bf16[8,128,256]{2,1,0:T(8,128)(2,1)S(1)} %get-tuple-element.82), channel_id=1, source_target_pairs={{0,6},{2,0},{4,2},{6,4},{1,7},{3,1},{5,3},{7,5},{8,14},{10,8},{12,... | collective-permute-start | bytes 1572872 | tf_op jit(solution)/shard_map/ppermute | solution.py:308
  52.2 4.1 %terms.7 = (bf16[512,128]{1,0:T(8,128)(2,1)S(1)}, bf16[512,128]{1,0:T(8,128)(2,1)S(1)}, bf16[512,128]{1,0:T(8,128)(2,1)S(1)}, bf16[512,128]{1,0:T(8,128)(2,1)S(1...) custom-call(s32[2]{0:T(128)S(1)} %pad_add_fusion.where_ref, ...), custom_call_target="tpu_custom_call" | custom-call | flops 2684354560 | bytes 3457024 | tf_op jit(solution)/shard_map/terms/pallas_call | solution.py:226
  56.7 1.5 %collective-permute-start.13 = (bf16[512,128]{1,0:T(8,128)(2,1)S(1)}, bf16[512,128]{1,0:T(8,128)(2,1)S(1)}, u32[]{:S(2)}, u32[]{:S(2)}) collective-permute-start(bf16[512,128]{1,0:T(8,128)(2,1)S(1)} %get-tuple-element.86), channel_id=1, source_target_pairs={{0,24},{1,25},{8,16},{9,17},{16,8},{17,9},{24,0},{25,1},{2,26},{3,... | collective-permute-start | bytes 393224 | tf_op jit(solution)/shard_map/ppermute | solution.py:305
  58.2 1.5 %collective-permute-start.14 = (bf16[512,128]{1,0:T(8,128)(2,1)S(1)}, bf16[512,128]{1,0:T(8,128)(2,1)S(1)}, u32[]{:S(2)}, u32[]{:S(2)}) collective-permute-start(bf16[512,128]{1,0:T(8,128)(2,1)S(1)} %get-tuple-element.87), channel_id=1, source_target_pairs={{0,1},{1,0},{8,9},{9,8},{16,17},{17,16},{24,25},{25,24},{2,3},{3,2... | collective-permute-start | bytes 393224 | tf_op jit(solution)/shard_map/ppermute | solution.py:305
  59.8 3.3 %collective-permute-done.12.refs_2_ = bf16[512,128]{1,0:T(8,128)(2,1)S(1)} collective-permute-done((bf16[512,128]{1,0:T(8,128)(2,1)S(1)}, bf16[512,128]{1,0:T(8,128)(2,1)S(1)}, u32[]{:S(2)}, u32[]{:S(2)}) %collective-permute-start.12) | collective-permute-done | bytes 131104 | tf_op jit(solution)/shard_map/ppermute | solution.py:305
  63.0 1.3 %collective-permute-done.13.refs_3_ = bf16[512,128]{1,0:T(8,128)(2,1)S(1)} collective-permute-done((bf16[512,128]{1,0:T(8,128)(2,1)S(1)}, bf16[512,128]{1,0:T(8,128)(2,1)S(1)}, u32[]{:S(2)}, u32[]{:S(2)}) %collective-permute-start.13) | collective-permute-done | bytes 131104 | tf_op jit(solution)/shard_map/ppermute | solution.py:305
  64.4 1.7 %collective-permute-start.16 = (bf16[512,128]{1,0:T(8,128)(2,1)S(1)}, bf16[512,128]{1,0:T(8,128)(2,1)S(1)}, u32[]{:S(2)}, u32[]{:S(2)}) collective-permute-start(bf16[512,128]{1,0:T(8,128)(2,1)S(1)} %get-tuple-element.89), channel_id=1, source_target_pairs={{0,17},{1,16},{8,25},{9,24},{16,1},{17,0},{24,9},{25,8},{2,19},{3,... | collective-permute-start | bytes 393224 | tf_op jit(solution)/shard_map/ppermute | solution.py:305
  66.0 1.1 %collective-permute-start.17 = (bf16[512,128]{1,0:T(8,128)(2,1)S(1)}, bf16[512,128]{1,0:T(8,128)(2,1)S(1)}, u32[]{:S(2)}, u32[]{:S(2)}) collective-permute-start(bf16[512,128]{1,0:T(8,128)(2,1)S(1)} %get-tuple-element.90), channel_id=1, source_target_pairs={{0,25},{1,24},{8,17},{9,16},{16,9},{17,8},{24,1},{25,0},{2,27},{3,... | collective-permute-start | bytes 393224 | tf_op jit(solution)/shard_map/ppermute | solution.py:305
  67.2 7.0 %collective-permute-done.15.refs_5_ = bf16[512,128]{1,0:T(8,128)(2,1)S(1)} collective-permute-done((bf16[512,128]{1,0:T(8,128)(2,1)S(1)}, bf16[512,128]{1,0:T(8,128)(2,1)S(1)}, u32[]{:S(2)}, u32[]{:S(2)}) %collective-permute-start.15) | collective-permute-done | bytes 131104 | tf_op jit(solution)/shard_map/ppermute | solution.py:305
  74.2 2.5 %collective-permute-done.10 = bf16[4,128,256]{2,1,0:T(8,128)(2,1)S(1)} collective-permute-done((bf16[4,128,256]{2,1,0:T(8,128)(2,1)S(1)}, bf16[4,128,256]{2,1,0:T(8,128)(2,1)S(1)}, u32[]{:S(2)}, u32[]{:S(2)}) %collective-permute-start.10) | collective-permute-done | bytes 262176 | tf_op jit(solution)/shard_map/ppermute | solution.py:308
  76.7 1.0 %multiply_convert_fusion = bf16[8,128,256]{2,1,0:T(8,128)(2,1)} fusion(f32[8,128,256]{2,1,0:T(8,128)S(1)} %get-tuple-element.98, bf16[8,128,256]{2,1,0:T(8,128)(2,1)S(1)} %collective-permute-done.9, f32[256]{0:T(256)S(1)} %compare_select_fusion, bf16[4,128,256]{2,1,0:T(8,128)(2,1)S(1)} %collective-permute-done.10), kind=kLoop, calls=%fused_computation | loop fusion | flops 1572864 | bytes 2360320 | tf_op jit(solution)/shard_map/convert_element_type | solution.py:247
  77.7 3.5 %all-to-all-start.1 = ((bf16[8,128,256]{2,1,0:T(8,128)(2,1)}), bf16[8,128,256]{2,1,0:T(8,128)(2,1)S(1)}, u32[]{:S(2)}, u32[]{:S(2)}) async-start(bf16[8,128,256]{2,1,0:T(8,128)(2,1)} %multiply_convert_fusion), calls=%async_computation.1 | async-start | bytes 1048576 | tf_op jit(solution)/shard_map/all_to_all | solution.py:311
  81.2 1.2 %unpack_queries.1 = bf16[128,4096]{1,0:T(8,128)(2,1)} custom-call(s32[1]{0:T(128)} %bitcast.me_ref, bf16[512,128]{1,0:T(8,128)(2,1)S(1)} %get-tuple-element.81.refs_0_, bf16[512,128]{1,0:T(8,128)(2,1)S(1)} %collective-permute-done.11.refs_1_, bf16[512,128]{1,0:T(8,128)(2,1)S(1)} %collective-permute-done.12.refs_2_, ...), custom_call_target="tpu_custom_call" | custom-call | tf_op jit(solution)/shard_map/unpack_queries/pallas_call | solution.py:262
  82.4 8.4 %all-to-all-done.1.in_ref = bf16[8,128,256]{2,1,0:T(8,128)(2,1)S(1)} async-done(((bf16[8,128,256]{2,1,0:T(8,128)(2,1)}), bf16[8,128,256]{2,1,0:T(8,128)(2,1)S(1)}, u32[]{:S(2)}, u32[]{:S(2)}) %all-to-all-start.1) | async-done | bytes 524320 | tf_op jit(solution)/shard_map/all_to_all | solution.py:311
  90.9 0.9 %unpack_kv.1 = (bf16[128,1024]{1,0:T(8,128)(2,1)}, bf16[128,1024]{1,0:T(8,128)(2,1)}) custom-call(bf16[8,128,256]{2,1,0:T(8,128)(2,1)S(1)} %all-to-all-done.1.in_ref), custom_call_target="tpu_custom_call" | custom-call | tf_op jit(solution)/shard_map/unpack_kv/pallas_call | solution.py:280
  (27 shorter events, 2.5 us)
Async XLA Ops:
  2.6 15.7 %all-to-all-start = ((bf16[8,272,128]{2,1,0:T(8,128)(2,1)}), bf16[8,272,128]{2,1,0:T(8,128)(2,1)S(1)}, u32[]{:S(2)}, u32[]{:S(2)}) async-start(bf16[8,272,128]{2,1,0:T(8,128)(2,1)} %pack_kv.1), calls=%async_computation | async-start | bytes 1114112 | tf_op jit(solution)/shard_map/all_to_all | solution.py:311
  12.2 3.7 %collective-permute-start = (bf16[1040,128]{1,0:T(8,128)(2,1)}, bf16[1040,128]{1,0:T(8,128)(2,1)S(1)}, u32[]{:S(2)}, u32[]{:S(2)}) collective-permute-start(bf16[1040,128]{1,0:T(8,128)(2,1)} %get-tuple-element.53), channel_id=1, source_target_pairs={{0,8},{1,9},{8,0},{9,1},{16,24},{17,25},{24,16},{25,17},{2,10},{3,... | collective-permute-start | bytes 798728 | tf_op jit(solution)/shard_map/ppermute | solution.py:305
  12.8 10.0 %collective-permute-start.1 = (bf16[1040,128]{1,0:T(8,128)(2,1)}, bf16[1040,128]{1,0:T(8,128)(2,1)S(1)}, u32[]{:S(2)}, u32[]{:S(2)}) collective-permute-start(bf16[1040,128]{1,0:T(8,128)(2,1)} %get-tuple-element.59), channel_id=1, source_target_pairs={{0,16},{1,17},{8,24},{9,25},{16,0},{17,1},{24,8},{25,9},{2,18},{3,... | collective-permute-start | bytes 798728 | tf_op jit(solution)/shard_map/ppermute | solution.py:305
  14.4 9.5 %collective-permute-start.2 = (bf16[1040,128]{1,0:T(8,128)(2,1)}, bf16[1040,128]{1,0:T(8,128)(2,1)S(1)}, u32[]{:S(2)}, u32[]{:S(2)}) collective-permute-start(bf16[1040,128]{1,0:T(8,128)(2,1)} %get-tuple-element.60), channel_id=1, source_target_pairs={{0,1},{1,0},{8,9},{9,8},{16,17},{17,16},{24,25},{25,24},{2,3},{3,2... | collective-permute-start | bytes 798728 | tf_op jit(solution)/shard_map/ppermute | solution.py:305
  18.3 13.8 %collective-permute-start.8 = (bf16[8,272,128]{2,1,0:T(8,128)(2,1)S(1)}, bf16[8,272,128]{2,1,0:T(8,128)(2,1)S(1)}, u32[]{:S(2)}, u32[]{:S(2)}) collective-permute-start(bf16[8,272,128]{2,1,0:T(8,128)(2,1)S(1)} %all-to-all-done.refs_4_), channel_id=1, source_target_pairs={{0,2},{2,4},{4,6},{6,0},{1,3},{3,5},{5,7},{7,1},{8,10},{10,12},{12... | collective-permute-start | bytes 1671176 | tf_op jit(solution)/shard_map/ppermute | solution.py:308
  19.9 18.6 %collective-permute-start.3 = (bf16[1040,128]{1,0:T(8,128)(2,1)}, bf16[1040,128]{1,0:T(8,128)(2,1)S(1)}, u32[]{:S(2)}, u32[]{:S(2)}) collective-permute-start(bf16[1040,128]{1,0:T(8,128)(2,1)} %get-tuple-element.62), channel_id=1, source_target_pairs={{0,24},{1,25},{8,16},{9,17},{16,8},{17,9},{24,0},{25,1},{2,26},{3,... | collective-permute-start | bytes 798728 | tf_op jit(solution)/shard_map/ppermute | solution.py:305
  19.9 19.4 %collective-permute-start.4 = (bf16[1040,128]{1,0:T(8,128)(2,1)}, bf16[1040,128]{1,0:T(8,128)(2,1)S(1)}, u32[]{:S(2)}, u32[]{:S(2)}) collective-permute-start(bf16[1040,128]{1,0:T(8,128)(2,1)} %get-tuple-element.64), channel_id=1, source_target_pairs={{0,9},{1,8},{8,1},{9,0},{16,25},{17,24},{24,17},{25,16},{2,11},{3,... | collective-permute-start | bytes 798728 | tf_op jit(solution)/shard_map/ppermute | solution.py:305
  23.9 15.4 %collective-permute-start.5 = (bf16[1040,128]{1,0:T(8,128)(2,1)}, bf16[1040,128]{1,0:T(8,128)(2,1)S(1)}, u32[]{:S(2)}, u32[]{:S(2)}) collective-permute-start(bf16[1040,128]{1,0:T(8,128)(2,1)} %get-tuple-element.65), channel_id=1, source_target_pairs={{0,17},{1,16},{8,25},{9,24},{16,1},{17,0},{24,9},{25,8},{2,19},{3,... | collective-permute-start | bytes 798728 | tf_op jit(solution)/shard_map/ppermute | solution.py:305
  25.6 14.7 %collective-permute-start.6 = (bf16[1040,128]{1,0:T(8,128)(2,1)}, bf16[1040,128]{1,0:T(8,128)(2,1)S(1)}, u32[]{:S(2)}, u32[]{:S(2)}) collective-permute-start(bf16[1040,128]{1,0:T(8,128)(2,1)} %get-tuple-element.66), channel_id=1, source_target_pairs={{0,25},{1,24},{8,17},{9,16},{16,9},{17,8},{24,1},{25,0},{2,27},{3,... | collective-permute-start | bytes 798728 | tf_op jit(solution)/shard_map/ppermute | solution.py:305
  25.6 1.0 %copy-start = (bf16[1040,128]{1,0:T(8,128)(2,1)S(1)}, bf16[1040,128]{1,0:T(8,128)(2,1)}, u32[]{:S(2)}) copy-start(bf16[1040,128]{1,0:T(8,128)(2,1)} %get-tuple-element.55.refs_0_) | copy-start | bytes 798724
  26.7 5.4 %copy-start.1 = (bf16[4,272,128]{2,1,0:T(8,128)(2,1)S(1)}, bf16[4,272,128]{2,1,0:T(8,128)(2,1)}, u32[]{:S(2)}) copy-start(bf16[4,272,128]{2,1,0:T(8,128)(2,1)} %slice.7) | copy-start | bytes 835588
  32.1 20.1 %collective-permute-start.7 = (bf16[4,272,128]{2,1,0:T(8,128)(2,1)S(1)}, bf16[4,272,128]{2,1,0:T(8,128)(2,1)S(1)}, u32[]{:S(2)}, u32[]{:S(2)}) collective-permute-start(bf16[4,272,128]{2,1,0:T(8,128)(2,1)S(1)} %copy-done.1), channel_id=1, source_target_pairs={{0,4},{2,6},{4,0},{6,2},{1,5},{3,7},{5,1},{7,3},{8,12},{10,14},{12... | collective-permute-start | bytes 835592 | tf_op jit(solution)/shard_map/ppermute | solution.py:308
  49.4 27.3 %collective-permute-start.9 = (bf16[8,128,256]{2,1,0:T(8,128)(2,1)S(1)}, bf16[8,128,256]{2,1,0:T(8,128)(2,1)S(1)}, u32[]{:S(2)}, u32[]{:S(2)}) collective-permute-start(bf16[8,128,256]{2,1,0:T(8,128)(2,1)S(1)} %get-tuple-element.82), channel_id=1, source_target_pairs={{0,6},{2,0},{4,2},{6,4},{1,7},{3,1},{5,3},{7,5},{8,14},{10,8},{12,... | collective-permute-start | bytes 1572872 | tf_op jit(solution)/shard_map/ppermute | solution.py:308
  56.3 3.4 %collective-permute-start.11 = (bf16[512,128]{1,0:T(8,128)(2,1)S(1)}, bf16[512,128]{1,0:T(8,128)(2,1)S(1)}, u32[]{:S(2)}, u32[]{:S(2)}) collective-permute-start(bf16[512,128]{1,0:T(8,128)(2,1)S(1)} %get-tuple-element.84), channel_id=1, source_target_pairs={{0,8},{1,9},{8,0},{9,1},{16,24},{17,25},{24,16},{25,17},{2,10},{3,... | collective-permute-start | bytes 393224 | tf_op jit(solution)/shard_map/ppermute | solution.py:305
  56.7 6.3 %collective-permute-start.12 = (bf16[512,128]{1,0:T(8,128)(2,1)S(1)}, bf16[512,128]{1,0:T(8,128)(2,1)S(1)}, u32[]{:S(2)}, u32[]{:S(2)}) collective-permute-start(bf16[512,128]{1,0:T(8,128)(2,1)S(1)} %get-tuple-element.85), channel_id=1, source_target_pairs={{0,16},{1,17},{8,24},{9,25},{16,0},{17,1},{24,8},{25,9},{2,18},{3,... | collective-permute-start | bytes 393224 | tf_op jit(solution)/shard_map/ppermute | solution.py:305
  56.7 7.7 %collective-permute-start.13 = (bf16[512,128]{1,0:T(8,128)(2,1)S(1)}, bf16[512,128]{1,0:T(8,128)(2,1)S(1)}, u32[]{:S(2)}, u32[]{:S(2)}) collective-permute-start(bf16[512,128]{1,0:T(8,128)(2,1)S(1)} %get-tuple-element.86), channel_id=1, source_target_pairs={{0,24},{1,25},{8,16},{9,17},{16,8},{17,9},{24,0},{25,1},{2,26},{3,... | collective-permute-start | bytes 393224 | tf_op jit(solution)/shard_map/ppermute | solution.py:305
  58.2 7.8 %collective-permute-start.14 = (bf16[512,128]{1,0:T(8,128)(2,1)S(1)}, bf16[512,128]{1,0:T(8,128)(2,1)S(1)}, u32[]{:S(2)}, u32[]{:S(2)}) collective-permute-start(bf16[512,128]{1,0:T(8,128)(2,1)S(1)} %get-tuple-element.87), channel_id=1, source_target_pairs={{0,1},{1,0},{8,9},{9,8},{16,17},{17,16},{24,25},{25,24},{2,3},{3,2... | collective-permute-start | bytes 393224 | tf_op jit(solution)/shard_map/ppermute | solution.py:305
  59.7 17.0 %collective-permute-start.10 = (bf16[4,128,256]{2,1,0:T(8,128)(2,1)S(1)}, bf16[4,128,256]{2,1,0:T(8,128)(2,1)S(1)}, u32[]{:S(2)}, u32[]{:S(2)}) collective-permute-start(bf16[4,128,256]{2,1,0:T(8,128)(2,1)S(1)} %get-tuple-element.83), channel_id=1, source_target_pairs={{0,4},{2,6},{4,0},{6,2},{1,5},{3,7},{5,1},{7,3},{8,12},{10,14},{12... | collective-permute-start | bytes 786440 | tf_op jit(solution)/shard_map/ppermute | solution.py:308
  63.0 11.2 %collective-permute-start.15 = (bf16[512,128]{1,0:T(8,128)(2,1)S(1)}, bf16[512,128]{1,0:T(8,128)(2,1)S(1)}, u32[]{:S(2)}, u32[]{:S(2)}) collective-permute-start(bf16[512,128]{1,0:T(8,128)(2,1)S(1)} %get-tuple-element.88), channel_id=1, source_target_pairs={{0,9},{1,8},{8,1},{9,0},{16,25},{17,24},{24,17},{25,16},{2,11},{3,... | collective-permute-start | bytes 393224 | tf_op jit(solution)/shard_map/ppermute | solution.py:305
  64.4 9.8 %collective-permute-start.16 = (bf16[512,128]{1,0:T(8,128)(2,1)S(1)}, bf16[512,128]{1,0:T(8,128)(2,1)S(1)}, u32[]{:S(2)}, u32[]{:S(2)}) collective-permute-start(bf16[512,128]{1,0:T(8,128)(2,1)S(1)} %get-tuple-element.89), channel_id=1, source_target_pairs={{0,17},{1,16},{8,25},{9,24},{16,1},{17,0},{24,9},{25,8},{2,19},{3,... | collective-permute-start | bytes 393224 | tf_op jit(solution)/shard_map/ppermute | solution.py:305
  66.0 8.2 %collective-permute-start.17 = (bf16[512,128]{1,0:T(8,128)(2,1)S(1)}, bf16[512,128]{1,0:T(8,128)(2,1)S(1)}, u32[]{:S(2)}, u32[]{:S(2)}) collective-permute-start(bf16[512,128]{1,0:T(8,128)(2,1)S(1)} %get-tuple-element.90), channel_id=1, source_target_pairs={{0,25},{1,24},{8,17},{9,16},{16,9},{17,8},{24,1},{25,0},{2,27},{3,... | collective-permute-start | bytes 393224 | tf_op jit(solution)/shard_map/ppermute | solution.py:305
  77.7 13.2 %all-to-all-start.1 = ((bf16[8,128,256]{2,1,0:T(8,128)(2,1)}), bf16[8,128,256]{2,1,0:T(8,128)(2,1)S(1)}, u32[]{:S(2)}, u32[]{:S(2)}) async-start(bf16[8,128,256]{2,1,0:T(8,128)(2,1)} %multiply_convert_fusion), calls=%async_computation.1 | async-start | bytes 1048576 | tf_op jit(solution)/shard_map/all_to_all | solution.py:311
